TPU v7x, 32 devices: a whole 2x2x4 slice. The times are simulated.
32 devices in a mesh: wide: 8 (over z, y), narrow: 4 (over x, core).
Axes of the slice: x: 2, y: 2, z: 4, core: 2. Of those that a mesh axis runs over, the one named last changes fastest.
Arguments:
- tokens: bfloat16 [8192, 1024], P('wide'), may hold values from -6 to 6
- gain_in: bfloat16 [1024], replicated, may hold values from 0.5 to 1.5
- gain_mid: bfloat16 [1024], replicated, may hold values from 0.5 to 1.5
- w_qkv: bfloat16 [1024, 3, 1024], P(None, None, 'narrow'), may hold values from -0.1875 to 0.1875
- w_gate: bfloat16 [1024, 16], replicated, may hold values from -0.1875 to 0.1875
- w_decay: bfloat16 [1024, 2], replicated, may hold values from -0.1875 to 0.1875
- conv_kernel: bfloat16 [3, 4, 1024], P(None, None, 'narrow'), may hold values from -3 to 3
- persistent: bfloat16 [2, 16, 1024], P(None, None, 'narrow'), may hold values from -1.5 to 1.5
- w_out: bfloat16 [1024, 1024], P('narrow'), may hold values from -0.5 to 0.5
- mem_in: bfloat16 [1024, 4096], P(None, 'narrow'), may hold values from -1.5 to 1.5
- mem_out: bfloat16 [4096, 1024], P('narrow'), may hold values from -0.09375 to 0.09375
- w_up: bfloat16 [1024, 2, 4096], P(None, None, 'narrow'), may hold values from -0.1875 to 0.1875
- w_down: bfloat16 [4096, 1024], P('narrow'), may hold values from -0.09375 to 0.09375
- doc_len: int32 [8, 8], P('wide'), may hold values from 1 to 512, 1024 in all within a row
- reset: int32 [8], P('wide'), may hold values 0 or 1
- cotangent: bfloat16 [8192, 1024], P('wide', 'narrow'), may hold values from -6 to 6
Outputs:
- output: bfloat16 [8192, 1024], P('wide', 'narrow')
- grad_input: float32 [8192, 1024], P('wide', 'narrow')
- grad_gain_in: float32 [1024], replicated
- grad_gain_mid: float32 [1024], replicated
- grad_w_qkv: float32 [1024, 3, 1024], P('wide', None, 'narrow')
- grad_w_gate: float32 [1024, 16], P('wide')
- grad_w_decay: float32 [1024, 2], replicated
- grad_conv: float32 [3, 4, 1024], replicated
- grad_persistent: float32 [2, 16, 1024], replicated
- grad_w_out: float32 [1024, 1024], P('narrow', 'wide')
- grad_mem_in: float32 [1024, 4096], P('wide', 'narrow')
- grad_mem_out: float32 [4096, 1024], P('narrow', 'wide')
- grad_w_up: float32 [1024, 2, 4096], P('wide', None, 'narrow')
- grad_w_down: float32 [4096, 1024], P('narrow', 'wide')
Inputs may be any that keep to these rules, and one draw needn't show every extreme that they name: `doc_len`: in each row the 8 lengths sum to 1024, and the longest is exactly 512.
All inputs are finite; a program needn't handle non-finite values. No bound on the sum of `reset` on one device may be relied on, other than what follows from the above.
Results may differ from a plain program's by a relative error of at most 0.014.
Values may be sent and summed in bfloat16 or wider, within the bound.
No kernel may reach another device: no remote copies, remote signals or barrier semaphores. Data moves between devices by JAX's collectives and lax.ppermute only.
A program may use at most 256 MiB of HBM per device.

v0:
```python
import jax
import jax.numpy as jnp
from jax import lax
from jax.sharding import PartitionSpec as P

D = 1024
HEADS = 16
HD = 64
LEN = 1024
CH = 512
WIN = 512
NP = 16
KC = 4


EPS = 1e-06
NEG = -1e30
STEP_IN = 128.0
STEP_OUT = 0.5
HIGHEST = lax.Precision.HIGHEST


def segment_ids(lengths):
    doc_ends = jnp.cumsum(lengths)
    places = jnp.arange(LEN, dtype=jnp.int32)
    return jnp.sum((places[:, None] >= doc_ends[None, :]).astype(jnp.int32), axis=1)


def mix_inputs(projected, kernel, segment):
    feat_width = projected.shape[2]
    summed = kernel[:, 0][None] * projected
    for offset in range(1, KC):
        shifted = jnp.concatenate(
            [jnp.zeros((offset, 3, feat_width), projected.dtype), projected[:-offset]], 0
        )
        same_doc = jnp.concatenate(
            [jnp.zeros((offset,), jnp.bool_), segment[offset:] == segment[:-offset]], 0
        )
        summed = summed + kernel[:, offset][None] * jnp.where(same_doc[:, None, None], shifted, 0.0)
    active = jax.nn.silu(summed)
    paired = active[:, :2].reshape(LEN, 2, feat_width // HD, HD)
    paired = paired * lax.rsqrt(jnp.sum(paired * paired, -1, keepdims=True) + EPS)
    return jnp.concatenate([paired.reshape(LEN, 2, feat_width), active[:, 2:]], 1)


def product(formula, left_op, right_op):
    return jnp.einsum(formula, left_op, right_op, preferred_element_type=jnp.float32)


def precise(formula, left_op, right_op):
    return jnp.einsum(
        formula, left_op, right_op, precision=HIGHEST, preferred_element_type=jnp.float32
    )


def norm_back(grad_norm, unit_val, inverse, gain_vec):
    scaled = grad_norm * gain_vec
    return inverse * (scaled - unit_val * jnp.mean(scaled * unit_val, -1, keepdims=True))


def swish_parts(pre_act):
    sig_val = jax.nn.sigmoid(pre_act)
    return (sig_val, sig_val * (1.0 + pre_act * (1.0 - sig_val)))


def window_mask(segments, block_start):
    places = jnp.arange(LEN, dtype=jnp.int32)
    query_pos = block_start + jnp.arange(CH, dtype=jnp.int32)
    query_seg = segments[:, block_start : block_start + CH]
    return (
        (places[None, None, :] <= query_pos[None, :, None])
        & (query_pos[None, :, None] - places[None, None, :] < WIN)
        & (segments[:, None, :] == query_seg[:, :, None])
    )


def body(
    tokens,
    gain_in,
    gain_mid,
    w_qkv,
    w_gate,
    w_decay,
    conv_kernel,
    persistent,
    w_out,
    mem_in,
    mem_out,
    w_up,
    w_down,
    doc_len,
    reset,
    cotangent,
):
    rows_here = doc_len.shape[0]
    local_width = w_qkv.shape[2]
    local_heads = local_width // HD
    ffn_width = w_up.shape[2]
    token_count = rows_here * LEN
    lead_col = lax.axis_index("narrow") * local_width
    first_dev = (lax.axis_index("narrow") == 0).astype(jnp.float32)
    score_scale = HD**0.5
    segments = jax.vmap(segment_ids)(doc_len)
    keep_rows = 1.0 - reset.astype(jnp.float32)
    gain_in_f = gain_in.astype(jnp.float32)
    gain_mid_f = gain_mid.astype(jnp.float32)
    mem_in_f = mem_in.astype(jnp.float32)
    mem_out_f = mem_out.astype(jnp.float32)
    inputs = tokens.astype(jnp.float32)
    inverse_in = lax.rsqrt(jnp.mean(inputs * inputs, -1, keepdims=True) + EPS)
    unit_in = inputs * inverse_in
    normed_in = (unit_in * gain_in_f).astype(jnp.bfloat16)
    projected = jnp.dot(
        normed_in, w_qkv.reshape(D, 3 * local_width), preferred_element_type=jnp.float32
    ).reshape(rows_here, LEN, 3, local_width)

    def mixing(proj_in, kernel):
        return jax.vmap(mix_inputs, (0, None, 0))(proj_in, kernel, segments)

    mixed_act, mixing_back = jax.vjp(mixing, projected, conv_kernel.astype(jnp.float32))
    act_low = mixed_act.astype(jnp.bfloat16)
    full_act = lax.all_gather(act_low, "narrow", axis=3, tiled=True)
    mem_gates = jax.nn.sigmoid(
        jnp.dot(normed_in, w_decay, preferred_element_type=jnp.float32)
    ).reshape(rows_here, LEN, 2)
    decay_row = jnp.mean(mem_gates[:, :CH, 0], axis=1)
    step_rate = jnp.mean(mem_gates[:, :CH, 1], axis=1)
    key_block = full_act[:, :CH, 1]
    value_block = full_act[:, :CH, 2]
    key_pre = product("rcd,df->rcf", key_block, mem_in)
    key_sig, key_slope = swish_parts(key_pre)
    key_hidden = (key_pre * key_sig).astype(jnp.bfloat16)
    predicted = lax.psum(product("rcf,fd->rcd", key_hidden, mem_out), "narrow")
    error_low = (predicted - value_block.astype(jnp.float32)).astype(jnp.bfloat16)
    back_hidden = product("rcd,fd->rcf", error_low, mem_out)
    slope_low = (back_hidden * key_slope).astype(jnp.bfloat16)
    grad_in = product("rcd,rcf->rdf", key_block, slope_low) / CH
    grad_out = product("rcf,rcd->rfd", key_hidden, error_low) / CH
    keep_col = keep_rows[:, None, None]
    rate_col = step_rate[:, None, None]
    decay_col = decay_row[:, None, None]
    memory_in = mem_in_f[None] - keep_col * (
        decay_col * mem_in_f[None] + rate_col * STEP_IN * grad_in
    )
    memory_out = mem_out_f[None] - keep_col * (
        decay_col * mem_out_f[None] + rate_col * STEP_OUT * grad_out
    )
    memory_in_low = memory_in.astype(jnp.bfloat16)
    memory_out_low = memory_out.astype(jnp.bfloat16)
    query_all = full_act[:, :, 0]
    first_pre = product("rcd,df->rcf", query_all[:, :CH], mem_in)
    second_pre = product("rcd,rdf->rcf", query_all[:, CH:], memory_in_low)
    first_sig, first_slope = swish_parts(first_pre)
    second_sig, second_slope = swish_parts(second_pre)
    first_hidden = (first_pre * first_sig).astype(jnp.bfloat16)
    second_hidden = (second_pre * second_sig).astype(jnp.bfloat16)
    recall_part = jnp.concatenate(
        [
            product("rcf,fd->rcd", first_hidden, mem_out),
            product("rcf,rfd->rcd", second_hidden, memory_out_low),
        ],
        1,
    )
    query_loc = act_low[:, :, 0].reshape(rows_here, LEN, local_heads, HD)
    key_loc = act_low[:, :, 1].reshape(rows_here, LEN, local_heads, HD)
    value_loc = act_low[:, :, 2].reshape(rows_here, LEN, local_heads, HD)
    pers_keys = persistent[0].reshape(NP, local_heads, HD)
    pers_values = persistent[1].reshape(NP, local_heads, HD)

    def block_scores(block_start):
        query_blk = query_loc[:, block_start : block_start + CH]
        allowed = window_mask(segments, block_start)[:, None]
        scores = jnp.where(
            allowed, score_scale * product("rqhd,rkhd->rhqk", query_blk, key_loc), NEG
        )
        pers_scores = score_scale * product("rqhd,khd->rhqk", query_blk, pers_keys)
        return (query_blk, scores, pers_scores)

    peak_list = []
    normal_list = []
    out_list = []
    for block_start in range(0, LEN, CH):
        query_blk, scores, pers_scores = block_scores(block_start)
        row_peak = jnp.maximum(jnp.max(scores, -1), jnp.max(pers_scores, -1))[..., None]
        weights = jnp.exp(scores - row_peak)
        pers_weights = jnp.exp(pers_scores - row_peak)
        normal = jnp.sum(weights, -1, keepdims=True) + jnp.sum(pers_weights, -1, keepdims=True)
        prob_low = (weights / normal).astype(jnp.bfloat16)
        pers_low = (pers_weights / normal).astype(jnp.bfloat16)
        out_list.append(
            product("rhqk,rkhd->rqhd", prob_low, value_loc)
            + product("rhqk,khd->rqhd", pers_low, pers_values)
        )
        peak_list.append(row_peak)
        normal_list.append(normal)
    attended = jnp.concatenate(out_list, 1).reshape(token_count, local_width).astype(jnp.bfloat16)
    mixed_part = jnp.dot(attended, w_out, preferred_element_type=jnp.float32)
    gate_act = jax.nn.sigmoid(jnp.dot(normed_in, w_gate, preferred_element_type=jnp.float32))
    gate_wide = jnp.repeat(gate_act, HD, axis=1)
    mixed_out, recalled = lax.psum((mixed_part, recall_part.reshape(token_count, D)), "narrow")
    middle = inputs + mixed_out + gate_wide * recalled
    inverse_mid = lax.rsqrt(jnp.mean(middle * middle, -1, keepdims=True) + EPS)
    unit_mid = middle * inverse_mid
    middle_local = lax.dynamic_slice_in_dim(middle, lead_col, local_width, 1)
    normed_mid = (unit_mid * gain_mid_f).astype(jnp.bfloat16)
    gate_up = jnp.dot(
        normed_mid, w_up.reshape(D, 2 * ffn_width), preferred_element_type=jnp.float32
    ).reshape(token_count, 2, ffn_width)
    gate_val = gate_up[:, 0]
    up_val = gate_up[:, 1]
    gate_sig = jax.nn.sigmoid(gate_val)
    hidden = (gate_val * gate_sig * up_val).astype(jnp.bfloat16)
    ffn_out = lax.psum_scatter(
        jnp.dot(hidden, w_down, preferred_element_type=jnp.float32).astype(jnp.bfloat16),
        "narrow",
        scatter_dimension=1,
        tiled=True,
    ).astype(jnp.float32)
    output = (middle_local + ffn_out).astype(jnp.bfloat16)
    grad_full = lax.all_gather(cotangent, "narrow", axis=1, tiled=True)
    grad_down = product("td,tf->df", grad_full, hidden)
    grad_hidden = product("td,fd->tf", grad_full, w_down)
    grad_pre_low = jnp.stack(
        [
            grad_hidden * up_val * gate_sig * (1.0 + gate_val * (1.0 - gate_sig)),
            grad_hidden * gate_val * gate_sig,
        ],
        1,
    ).astype(jnp.bfloat16)
    grad_up_w = product("td,tcf->dcf", normed_mid, grad_pre_low)
    grad_norm_mid = product("tcf,dcf->td", grad_pre_low, w_up)
    gain_mid_part = jnp.sum(grad_norm_mid * unit_mid, 0)
    grad_middle = lax.psum(
        norm_back(grad_norm_mid, unit_mid, inverse_mid, gain_mid_f), "narrow"
    ) + grad_full.astype(jnp.float32)
    grad_recalled = gate_wide * grad_middle
    gate_terms = jnp.sum((recalled * grad_middle).reshape(token_count, HEADS, HD), -1)
    grad_head_gate = gate_terms * gate_act * (1.0 - gate_act)
    normed_f = normed_in.astype(jnp.float32)
    grad_gate_w = precise("td,th->dh", normed_f, grad_head_gate)
    grad_norm_rep = jnp.dot(grad_head_gate, w_gate.astype(jnp.float32).T, precision=HIGHEST)
    grad_mixed_low = grad_middle.astype(jnp.bfloat16)
    grad_out_w = product("td,tf->df", grad_mixed_low, attended)
    grad_att_low = (
        product("td,fd->tf", grad_mixed_low, w_out)
        .astype(jnp.bfloat16)
        .reshape(rows_here, LEN, local_heads, HD)
    )
    grad_recall_low = grad_recalled.astype(jnp.bfloat16).reshape(rows_here, LEN, D)
    grad_query_list = []
    grad_key_att = jnp.zeros((rows_here, LEN, local_heads, HD), jnp.float32)
    grad_value_att = jnp.zeros((rows_here, LEN, local_heads, HD), jnp.float32)
    grad_pers_key = jnp.zeros((NP, local_heads, HD), jnp.float32)
    grad_pers_value = jnp.zeros((NP, local_heads, HD), jnp.float32)
    for block_index, block_start in enumerate(range(0, LEN, CH)):
        query_blk, scores, pers_scores = block_scores(block_start)
        prob_full = jnp.exp(scores - peak_list[block_index]) / normal_list[block_index]
        pers_probs = jnp.exp(pers_scores - peak_list[block_index]) / normal_list[block_index]
        grad_blk = grad_att_low[:, block_start : block_start + CH]
        grad_probs = product("rqhd,rkhd->rhqk", grad_blk, value_loc)
        grad_pers_probs = product("rqhd,khd->rhqk", grad_blk, pers_values)
        center = jnp.sum(prob_full * grad_probs, -1, keepdims=True) + jnp.sum(
            pers_probs * grad_pers_probs, -1, keepdims=True
        )
        grad_scores = (prob_full * (grad_probs - center)).astype(jnp.bfloat16)
        grad_pers_scores = (pers_probs * (grad_pers_probs - center)).astype(jnp.bfloat16)
        grad_query_list.append(
            score_scale
            * (
                product("rhqk,rkhd->rqhd", grad_scores, key_loc)
                + product("rhqk,khd->rqhd", grad_pers_scores, pers_keys)
            )
        )
        grad_key_att = grad_key_att + score_scale * product(
            "rhqk,rqhd->rkhd", grad_scores, query_blk
        )
        grad_value_att = grad_value_att + product(
            "rhqk,rqhd->rkhd", prob_full.astype(jnp.bfloat16), grad_blk
        )
        grad_pers_key = grad_pers_key + score_scale * product(
            "rhqk,rqhd->khd", grad_pers_scores, query_blk
        )
        grad_pers_value = grad_pers_value + product(
            "rhqk,rqhd->khd", pers_probs.astype(jnp.bfloat16), grad_blk
        )
    grad_query_att = jnp.concatenate(grad_query_list, 1).reshape(rows_here, LEN, local_width)
    grad_key_att = grad_key_att.reshape(rows_here, LEN, local_width)
    grad_value_att = grad_value_att.reshape(rows_here, LEN, local_width)
    first_grad = grad_recall_low[:, :CH]
    second_grad = grad_recall_low[:, CH:]
    grad_mem_out = product("rcd,rcf->df", first_grad, first_hidden)
    grad_first_pre = (product("rcd,fd->rcf", first_grad, mem_out) * first_slope).astype(
        jnp.bfloat16
    )
    grad_mem_in = product("rcd,rcf->df", query_all[:, :CH], grad_first_pre)
    grad_query_first = product("rcf,df->rcd", grad_first_pre, mem_in)
    grad_memory_out = product("rcf,rcd->rfd", second_hidden, second_grad)
    grad_second_pre = (product("rcd,rfd->rcf", second_grad, memory_out_low) * second_slope).astype(
        jnp.bfloat16
    )
    grad_memory_in = product("rcd,rcf->rdf", query_all[:, CH:], grad_second_pre)
    grad_query_second = product("rcf,rdf->rcd", grad_second_pre, memory_in_low)
    retain = 1.0 - keep_rows * decay_row
    grad_mem_in = grad_mem_in + precise("r,rdf->df", retain, grad_memory_in)
    grad_mem_out = grad_mem_out + precise("r,rfd->df", retain, grad_memory_out)
    decay_part = -keep_rows * (
        jnp.sum(mem_in_f[None] * grad_memory_in, (1, 2))
        + jnp.sum(mem_out_f[None] * grad_memory_out, (1, 2))
    )
    step_part = -keep_rows * (
        STEP_IN * jnp.sum(grad_in * grad_memory_in, (1, 2))
        + STEP_OUT * jnp.sum(grad_out * grad_memory_out, (1, 2))
    )
    factor = -(keep_rows * step_rate)[:, None, None]
    grad_gin = (factor * STEP_IN * grad_memory_in).astype(jnp.bfloat16)
    grad_gout = (factor * STEP_OUT * grad_memory_out).astype(jnp.bfloat16)
    grad_slope = product("rcd,rdf->rcf", key_block, grad_gin) / CH
    grad_key_block = product("rcf,rdf->rcd", slope_low, grad_gin) / CH
    grad_key_hidden = product("rcd,rfd->rcf", error_low, grad_gout) / CH
    grad_error = product("rcf,rfd->rcd", key_hidden, grad_gout) / CH
    key_curve = key_sig * (1.0 - key_sig) * (2.0 + key_pre * (1.0 - 2.0 * key_sig))
    grad_back_low = (grad_slope * key_slope).astype(jnp.bfloat16)
    grad_error = grad_error + product("rcf,fd->rcd", grad_back_low, mem_out)
    grad_mem_out = grad_mem_out + product("rcf,rcd->df", grad_back_low, error_low)
    grad_pred = lax.psum(grad_error.astype(jnp.bfloat16), "narrow").astype(jnp.float32)
    grad_pred_low = grad_pred.astype(jnp.bfloat16)
    grad_key_hidden = grad_key_hidden + product("rcd,fd->rcf", grad_pred_low, mem_out)
    grad_mem_out = grad_mem_out + product("rcd,rcf->df", grad_pred_low, key_hidden)
    grad_key_pre = (grad_key_hidden * key_slope + grad_slope * back_hidden * key_curve).astype(
        jnp.bfloat16
    )
    grad_mem_in = grad_mem_in + product("rcd,rcf->df", key_block, grad_key_pre)
    grad_key_block = grad_key_block + product("rcf,df->rcd", grad_key_pre, mem_in)
    grad_query_mem = jnp.concatenate([grad_query_first, grad_query_second], 1)
    query_share, key_share = (
        lax.psum_scatter(
            grad_query_mem.astype(jnp.bfloat16), "narrow", scatter_dimension=2, tiled=True
        ).astype(jnp.float32),
        lax.psum_scatter(
            grad_key_block.astype(jnp.bfloat16), "narrow", scatter_dimension=2, tiled=True
        ).astype(jnp.float32),
    )
    value_share = -lax.dynamic_slice_in_dim(grad_pred, lead_col, local_width, 2)
    tail_zeros = jnp.zeros((rows_here, LEN - CH, local_width), jnp.float32)
    grad_act = jnp.stack(
        [
            grad_query_att + query_share,
            grad_key_att + jnp.concatenate([key_share, tail_zeros], 1),
            grad_value_att + jnp.concatenate([value_share, tail_zeros], 1),
        ],
        2,
    )
    grad_proj, grad_conv = mixing_back(grad_act)
    grad_proj_low = grad_proj.reshape(token_count, 3 * local_width).astype(jnp.bfloat16)
    grad_qkv_w = product("td,tf->df", normed_in, grad_proj_low).reshape(D, 3, local_width)
    grad_norm_part = product("tf,df->td", grad_proj_low, w_qkv.reshape(D, 3 * local_width))
    gate_slopes = mem_gates * (1.0 - mem_gates)
    in_first = (jnp.arange(LEN) < CH).astype(jnp.float32)
    step_logit = (step_part[:, None] * gate_slopes[:, :, 1] * in_first[None] / CH).reshape(
        token_count
    )
    decay_logit = (decay_part[:, None] * gate_slopes[:, :, 0] * in_first[None] / CH).reshape(
        token_count
    )
    decay_w = w_decay.astype(jnp.float32)
    grad_norm_part = (
        grad_norm_part
        + step_logit[:, None] * decay_w[:, 1][None]
        + decay_logit[:, None] * decay_w[:, 0][None]
    )
    step_w = precise("td,t->d", normed_f, step_logit)
    decay_w_part = precise("td,t->d", normed_f, decay_logit)
    gain_in_part = jnp.sum(grad_norm_part * unit_in, 0) + first_dev * jnp.sum(
        grad_norm_rep * unit_in, 0
    )
    input_share = lax.psum_scatter(
        norm_back(grad_norm_part, unit_in, inverse_in, gain_in_f).astype(jnp.bfloat16),
        "narrow",
        scatter_dimension=1,
        tiled=True,
    ).astype(jnp.float32)
    replicated_back = norm_back(grad_norm_rep, unit_in, inverse_in, gain_in_f) + grad_middle
    conv_full = lax.dynamic_update_slice(
        jnp.zeros((3, KC, D), jnp.float32), grad_conv, (0, 0, lead_col)
    )
    pers_stack = jnp.stack(
        [grad_pers_key.reshape(NP, local_width), grad_pers_value.reshape(NP, local_width)]
    )
    pers_full = lax.dynamic_update_slice(
        jnp.zeros((2, NP, D), jnp.float32), pers_stack, (0, 0, lead_col)
    )
    gain_in_sum, gain_mid_sum, step_sum, decay_sum, conv_sum, pers_sum = lax.psum(
        (gain_in_part, gain_mid_part, step_w, decay_w_part, conv_full, pers_full),
        ("wide", "narrow"),
    )
    grad_input = input_share + lax.dynamic_slice_in_dim(replicated_back, lead_col, local_width, 1)
    grad_decay = jnp.stack([decay_sum, step_sum], 1)
    qkv_shard, gate_shard, out_shard, in_shard, back_shard, up_shard, down_shard = (
        lax.psum_scatter(grad_qkv_w, "wide", scatter_dimension=0, tiled=True),
        lax.psum_scatter(grad_gate_w, "wide", scatter_dimension=0, tiled=True),
        lax.psum_scatter(grad_out_w, "wide", scatter_dimension=0, tiled=True),
        lax.psum_scatter(grad_mem_in, "wide", scatter_dimension=0, tiled=True),
        lax.psum_scatter(grad_mem_out, "wide", scatter_dimension=0, tiled=True),
        lax.psum_scatter(grad_up_w, "wide", scatter_dimension=0, tiled=True),
        lax.psum_scatter(grad_down, "wide", scatter_dimension=0, tiled=True),
    )
    return (
        output,
        grad_input,
        gain_in_sum,
        gain_mid_sum,
        qkv_shard,
        gate_shard,
        grad_decay,
        conv_sum,
        pers_sum,
        out_shard.T,
        in_shard,
        back_shard.T,
        up_shard,
        down_shard.T,
    )


def solution(mesh):
    in_specs = (
        P("wide", None),
        P(),
        P(),
        P(None, None, "narrow"),
        P(),
        P(),
        P(None, None, "narrow"),
        P(None, None, "narrow"),
        P("narrow", None),
        P(None, "narrow"),
        P("narrow", None),
        P(None, None, "narrow"),
        P("narrow", None),
        P("wide", None),
        P("wide"),
        P("wide", "narrow"),
    )
    out_specs = (
        P("wide", "narrow"),
        P("wide", "narrow"),
        P(),
        P(),
        P("wide", None, "narrow"),
        P("wide", None),
        P(),
        P(),
        P(),
        P("narrow", "wide"),
        P("wide", "narrow"),
        P("narrow", "wide"),
        P("wide", None, "narrow"),
        P("narrow", "wide"),
    )
    return jax.shard_map(body, mesh=mesh, in_specs=in_specs, out_specs=out_specs, check_vma=False)
```

profile of v0, /device:TPU:0, one launch (start us, length us, event | category | flops | bytes accessed | tf_op | source)
XLA Modules:
  0.0 1565.6 jit_solution(15046635301182709020)
XLA Ops:
  24.4 8.6 fusion.40
  81.3 18.9 %all-gather.3.cloned.1.call-done = bf16[1,1024,3,1024]{3,1,2,0:T(8,128)(2,1)} async-done(((bf16[1,1024,3,256]{3,1,2,0:T(8,128)(2,1)}), bf16[1,1024,3,1024]{3,1,2,0:T(8,128)(2,1)}) %all-gather.3.cloned.1.call-update) | async-done | bytes 6291472 | tf_op jit(solution)/shard_map/all_gather | solution.py:122
  100.2 4.8 multiply_convert_fusion.14
  116.3 43.9 %all-reduce.25.cloned.1.call-done = f32[1,512,1024]{2,1,0:T(8,128)} async-done(((f32[1,512,1024]{2,1,0:T(8,128)}), f32[1,512,1024]{2,1,0:T(8,128)}) %all-reduce.25.cloned.1.call-update) | async-done | bytes 2097168 | tf_op jit(solution)/shard_map/psum | solution.py:133
  166.3 5.4 fusion.24
  189.2 5.5 copy.107
  194.7 5.6 copy.146
  200.2 6.4 copy.108
  206.7 129.6 %all-reduce.35.cloned.1.call-done = (f32[1024,1024]{1,0:T(8,128)}, f32[1024,1024]{1,0:T(8,128)}) async-done(((f32[1024,1024]{1,0:T(8,128)}, f32[1024,1024]{1,0:T(8,128)}), (f32[1024,1024]{1,0:T(8,128)}, f32[1024,1024]{1,0:T(8,128)})) %all-reduce.35.cloned.1.call-update) | async-done | bytes 8388624 | tf_op jit(solution)/shard_map/psum | solution.py:200
  336.3 6.3 multiply_reduce_fusion.5
  344.5 7.0 fusion.138
  351.5 9.3 all-gather.5.cloned.1.call-done
  360.8 8.3 fusion.67
  369.1 5.4 fusion.32
  377.6 85.4 %all-reduce.27.cloned.1.call-done = f32[1024,1024]{1,0:T(8,128)} async-done(((f32[1024,1024]{1,0:T(8,128)}), f32[1024,1024]{1,0:T(8,128)}) %all-reduce.27.cloned.1.call-update) | async-done | bytes 4194320 | tf_op jit(solution)/shard_map/psum | solution.py:233
  463.0 7.8 fusion.49
  480.9 5.0 multiply_convert_fusion.10
  490.1 35.9 %all-reduce.29.cloned.1.call-done = bf16[1,512,1024]{2,1,0:T(8,128)(2,1)} async-done(((bf16[1,512,1024]{2,1,0:T(8,128)(2,1)}), bf16[1,512,1024]{2,1,0:T(8,128)(2,1)}) %all-reduce.29.cloned.1.call-update) | async-done | bytes 1048592 | tf_op jit(solution)/shard_map/psum | solution.py:325
  530.8 4.0 fusion.47
  548.5 4.0 fusion.108
  555.2 5.3 convolution_convert_fusion
  560.5 7.0 mul.881
  570.7 6.5 fusion.54
  577.2 5.6 multiply_reduce_fusion
  582.8 6.2 multiply_reduce_fusion.1
  591.7 5.4 copy.123
  603.1 6.0 fusion.71
  611.8 7.4 multiply_convert_fusion
  620.2 5.2 multiply_convert_fusion.1
  661.4 4.2 add_add_fusion.1
  667.0 4.3 multiply_reduce_fusion.9
  678.7 3.9 fusion.180
  682.6 6.3 fusion.19
  690.3 5.6 fusion.16
  696.0 11.5 fusion.41
  713.6 6.6 convolution_bitcast_fusion
  724.3 4.6 add_add_fusion
  735.7 4.0 fusion.31
  740.0 5.0 fusion.52
  749.0 78.6 %all-reduce.33.cloned.1.call-done = (f32[1024]{0:T(1024)}, f32[1024]{0:T(1024)}, f32[1024,1]{0,1:T(1,128)}, f32[1024,1]{0,1:T(1,128)}, f32[3,4,1024]{2,1,0:T(4,128)}) async-done(((f32[1024]{0:T(1024)}, f32[1024]{0:T(1024)}, f32[1024,1]{0,1:T(1,128)}, f32[1024,1]{0,1:T(1,128)}, f32[3,4,1024]{2,1,0:T(4,128)}), (f32[1024]{0:T(1024)}, f32[1024]{0:T(1024)}, f32[1024,1]{0,1:T(1,128)}, f32[1024,1]{0,1:T(1,128)}, ...) | async-done | bytes 65552 | tf_op jit(solution)/shard_map/psum | solution.py:392
  828.8 33.8 %reduce-scatter.18.cloned.1.call-done = bf16[1024,256]{1,0:T(8,128)(2,1)} async-done(((bf16[1024,1024]{1,0:T(8,128)(2,1)}), bf16[1024,256]{1,0:T(8,128)(2,1)}) %reduce-scatter.18.cloned.1.call-update) | async-done | bytes 524304 | tf_op jit(solution)/shard_map/reduce_scatter | solution.py:376
  866.2 149.2 %reduce-scatter.30.cloned.1.call-done = f32[128,2,1024]{2,0,1:T(8,128)} async-done(((f32[1024,2,1024]{2,0,1:T(8,128)}), f32[128,2,1024]{2,0,1:T(8,128)}) %reduce-scatter.30.cloned.1.call-update) | async-done | bytes 1048592 | tf_op jit(solution)/shard_map/reduce_scatter | solution.py:404
  1018.4 125.4 %all-reduce.31.cloned.1.call-done = f32[2,16,1024]{2,1,0:T(8,128)} async-done(((f32[2,16,1024]{2,1,0:T(8,128)}), f32[2,16,1024]{2,1,0:T(8,128)}) %all-reduce.31.cloned.1.call-update) | async-done | bytes 131088 | tf_op jit(solution)/shard_map/psum | solution.py:392
  1143.8 56.7 %reduce-scatter.22.cloned.1.call-done = f32[128,16]{0,1:T(8,128)} async-done(((f32[1024,16]{0,1:T(8,128)}), f32[128,16]{0,1:T(8,128)}) %reduce-scatter.22.cloned.1.call-update) | async-done | bytes 8208 | tf_op jit(solution)/shard_map/reduce_scatter | solution.py:400
  1200.5 91.9 %reduce-scatter.32.cloned.1.call-done = f32[128,1024]{0,1:T(8,128)} async-done(((f32[1024,1024]{0,1:T(8,128)}), f32[128,1024]{0,1:T(8,128)}) %reduce-scatter.32.cloned.1.call-update) | async-done | bytes 524304 | tf_op jit(solution)/shard_map/reduce_scatter | solution.py:405
  1292.3 91.8 %reduce-scatter.26.cloned.1.call-done = f32[128,1024]{1,0:T(8,128)} async-done(((f32[1024,1024]{1,0:T(8,128)}), f32[128,1024]{1,0:T(8,128)}) %reduce-scatter.26.cloned.1.call-update) | async-done | bytes 524304 | tf_op jit(solution)/shard_map/reduce_scatter | solution.py:402
  1384.1 92.6 %reduce-scatter.28.cloned.1.call-done = f32[128,1024]{0,1:T(8,128)} async-done(((f32[1024,1024]{0,1:T(8,128)}), f32[128,1024]{0,1:T(8,128)}) %reduce-scatter.28.cloned.1.call-update) | async-done | bytes 524304 | tf_op jit(solution)/shard_map/reduce_scatter | solution.py:403
  1476.6 78.8 %reduce-scatter.20.cloned.1.call-done = f32[128,3,256]{2,0,1:T(8,128)} async-done(((f32[1024,3,256]{2,0,1:T(8,128)}), f32[128,3,256]{2,0,1:T(8,128)}) %reduce-scatter.20.cloned.1.call-update) | async-done | bytes 393232 | tf_op jit(solution)/shard_map/reduce_scatter | solution.py:399
  (551 shorter events, 228.7 us)
Async XLA Ops:
  7.2 353.6 %copy-start = (bf16[1024,1024]{1,0:T(8,128)(2,1)S(1)}, bf16[1024,1024]{1,0:T(8,128)(2,1)}, u32[]{:S(2)}) copy-start(bf16[1024,1024]{1,0:T(8,128)(2,1)} %param.28) | copy-start | bytes 6291460
  7.2 93.0 %all-gather.3.cloned.1.call-start = ((), (), s32[]{:S(2)}) async-start(), calls=%async_computation.11 | async-start | bytes 7864320 | tf_op jit(solution)/shard_map/all_gather | solution.py:122
  9.3 15.0 copy-start.131
  24.2 8.7 copy-start.117
  24.2 8.7 copy-start.125
  24.2 8.7 copy-start.119
  24.2 8.7 copy-start.121
  24.4 8.6 copy-start.134
  24.4 8.6 copy-start.137
  50.2 110.1 %all-reduce.25.cloned.1.call-start = ((), (), s32[]{:S(2)}) async-start(), calls=%async_computation.12 | async-start | bytes 4194304 | tf_op jit(solution)/shard_map/psum | solution.py:133
  53.2 25.1 %copy-start.93 = (bf16[16,4,64]{2,1,0:T(4,128)(2,1)}, bf16[16,4,64]{2,1,0:T(4,128)(2,1)S(1)}, u32[]{:S(2)}) copy-start(bf16[16,4,64]{2,1,0:T(4,128)(2,1)S(1)} %reshape_squeeze.13) | copy-start | bytes 24580
  53.3 14.7 copy-start.82
  62.1 12.8 copy-start.51
  63.8 8.5 copy-start.28
  63.8 11.4 copy-start.26
  65.5 9.4 copy-start.86
  68.2 10.1 copy-start.53
  108.7 227.6 %all-reduce.35.cloned.1.call-start = ((), (), s32[]{:S(2)}) async-start(), calls=%async_computation.29 | async-start | bytes 16777216 | tf_op jit(solution)/shard_map/psum | solution.py:200
  162.6 10.4 copy-start.30
  182.8 177.9 %all-gather.5.cloned.1.call-start = ((), (), s32[]{:S(2)}) async-start(), calls=%async_computation.14 | async-start | bytes 2621440 | tf_op jit(solution)/shard_map/all_gather | solution.py:220
  183.4 279.6 %all-reduce.27.cloned.1.call-start = ((), (), s32[]{:S(2)}) async-start(), calls=%async_computation.15 | async-start | bytes 8388608 | tf_op jit(solution)/shard_map/psum | solution.py:233
  183.6 190.9 %copy-start.78 = (f32[1024]{0:T(1024)}, f32[1024]{0:T(1024)S(1)}, u32[]{:S(2)}) copy-start(f32[1024]{0:T(1024)S(1)} %convert_element_type.252) | copy-start | bytes 12292
  342.6 31.9 %copy-start.80 = (f32[1024]{0:T(1024)}, f32[1024]{0:T(1024)S(1)}, u32[]{:S(2)}) copy-start(f32[1024]{0:T(1024)S(1)} %add_rsqrt_fusion.1) | copy-start | bytes 12292
  377.3 148.7 %all-reduce.29.cloned.1.call-start = ((), (), s32[]{:S(2)}) async-start(), calls=%async_computation.16 | async-start | bytes 2097152 | tf_op jit(solution)/shard_map/psum | solution.py:325
  477.6 9.5 copy-start.15
  489.7 154.5 %reduce-scatter.16.cloned.1.call-start = ((), (), s32[]{:S(2)}) async-start(), calls=%async_computation.18 | async-start | bytes 1310720 | tf_op jit(solution)/shard_map/reduce_scatter | solution.py:339
  540.0 109.0 %reduce-scatter.14.cloned.1.call-start = ((), (), s32[]{:S(2)}) async-start(), calls=%async_computation.17 | async-start | bytes 2621440 | tf_op jit(solution)/shard_map/reduce_scatter | solution.py:336
  548.4 196.6 %reduce-scatter.24.cloned.1.call-start = ((), (), s32[]{:S(2)}) async-start(), calls=%async_computation.23 | async-start | bytes 1179648 | tf_op jit(solution)/shard_map/reduce_scatter | solution.py:401
  552.5 194.1 %reduce-scatter.12.cloned.1.call-start = ((), (), s32[]{:S(2)}) async-start(), calls=%async_computation.13 | async-start | bytes 2621440 | tf_op jit(solution)/shard_map/reduce_scatter | solution.py:213
  560.5 267.1 %all-reduce.33.cloned.1.call-start = ((), (), s32[]{:S(2)}) async-start(), calls=%async_computation.28 | async-start | bytes 131072 | tf_op jit(solution)/shard_map/psum | solution.py:392
  567.6 9.6 slice-start
  568.4 14.4 copy-start.73
  570.7 12.1 slice-start.2
  591.7 9.9 copy-start.111
  611.7 8.4 slice-start.5
  690.3 172.4 %reduce-scatter.18.cloned.1.call-start = ((), (), s32[]{:S(2)}) async-start(), calls=%async_computation.19 | async-start | bytes 2621440 | tf_op jit(solution)/shard_map/reduce_scatter | solution.py:376
  695.9 319.4 %reduce-scatter.30.cloned.1.call-start = ((), (), s32[]{:S(2)}) async-start(), calls=%async_computation.26 | async-start | bytes 9437184 | tf_op jit(solution)/shard_map/reduce_scatter | solution.py:404
  707.5 436.2 %all-reduce.31.cloned.1.call-start = ((), (), s32[]{:S(2)}) async-start(), calls=%async_computation.22 | async-start | bytes 262144 | tf_op jit(solution)/shard_map/psum | solution.py:392
  711.8 488.7 %reduce-scatter.22.cloned.1.call-start = ((), (), s32[]{:S(2)}) async-start(), calls=%async_computation.21 | async-start | bytes 73728 | tf_op jit(solution)/shard_map/reduce_scatter | solution.py:400
  713.4 578.9 %reduce-scatter.32.cloned.1.call-start = ((), (), s32[]{:S(2)}) async-start(), calls=%async_computation.27 | async-start | bytes 4718592 | tf_op jit(solution)/shard_map/reduce_scatter | solution.py:405
  720.3 663.8 %reduce-scatter.26.cloned.1.call-start = ((), (), s32[]{:S(2)}) async-start(), calls=%async_computation.24 | async-start | bytes 4718592 | tf_op jit(solution)/shard_map/reduce_scatter | solution.py:402
  728.9 747.7 %reduce-scatter.28.cloned.1.call-start = ((), (), s32[]{:S(2)}) async-start(), calls=%async_computation.25 | async-start | bytes 4718592 | tf_op jit(solution)/shard_map/reduce_scatter | solution.py:403
  739.7 815.7 %reduce-scatter.20.cloned.1.call-start = ((), (), s32[]{:S(2)}) async-start(), calls=%async_computation.20 | async-start | bytes 3538944 | tf_op jit(solution)/shard_map/reduce_scatter | solution.py:399
  744.9 117.7 %copy-start.107 = (f32[1024]{0:T(1024)S(1)}, f32[1024]{0:T(1024)}, u32[]{:S(2)}) copy-start(f32[1024]{0:T(1024)} %copy-done.105) | copy-start | bytes 12292
  862.7 696.2 %copy-start.1 = (bf16[1024,1024]{1,0:T(8,128)(2,1)S(1)}, bf16[1024,1024]{1,0:T(8,128)(2,1)}, u32[]{:S(2)}) copy-start(bf16[1024,1024]{1,0:T(8,128)(2,1)} %param.28) | copy-start | bytes 6291460
  862.7 692.8 %copy-start.147 = (f32[1024]{0:T(1024)S(1)}, f32[1024]{0:T(1024)}, u32[]{:S(2)}) copy-start(f32[1024]{0:T(1024)} %get-tuple-element.147) | copy-start | bytes 12292
  862.7 693.4 %copy-start.146 = (f32[1024]{0:T(1024)S(1)}, f32[1024]{0:T(1024)}, u32[]{:S(2)}) copy-start(f32[1024]{0:T(1024)} %get-tuple-element.148) | copy-start | bytes 12292
  862.7 694.0 %copy-start.110 = (f32[3,4,1024]{2,1,0:T(4,128)S(1)}, f32[3,4,1024]{2,1,0:T(4,128)}, u32[]{:S(2)}) copy-start(f32[3,4,1024]{2,1,0:T(4,128)} %get-tuple-element.152) | copy-start | bytes 147460
  (146 other events, 561.0 us)
Sparse Core Ops, SparseCore 0:
  50.3 49.8 all-gather.2
  108.8 51.3 all-reduce.24
  182.9 153.2 all-reduce.34
  337.8 22.9 all-gather.4
  377.4 85.4 all-reduce.26
  489.8 36.1 all-reduce.28
  540.1 25.2 reduce-scatter.15
  568.0 31.4 reduce-scatter.13
  603.2 63.3 reduce-scatter.23
  669.0 30.4 reduce-scatter.11
  707.6 119.9 all-reduce.32
  830.1 32.5 reduce-scatter.17
  866.3 149.0 reduce-scatter.29
  1022.2 121.4 all-reduce.30
  1147.6 52.7 reduce-scatter.21
  1204.9 87.3 reduce-scatter.31
  1296.4 87.6 reduce-scatter.25
  1388.6 88.0 reduce-scatter.27
  1480.8 74.5 reduce-scatter.19
where the time goes:
time: 1570 us
  waiting for transfers between devices  1120 us (71%)
  matrix products  200 us (13%)
  other arithmetic  112 us (7%)
  local copies, waits for them, and re-layouts  109 us (7%)
  between operations  20.8 us (1%)
    psum x2, waiting for transfers between devices, body(): lax.psum((gain_in_part, gain_mid_part, step_w, decay_w_part, conv_full, p...  204 us
    dot_general x59, matrix products, product(): jnp.einsum(formula, left_op, right_op, preferred_element_type=jnp.float32)  166 us
    reduce_scatter x1, waiting for transfers between devices, body(): lax.psum_scatter(grad_up_w, 'wide', scatter_dimension=0, tiled=True)  149 us
    psum x1, waiting for transfers between devices, body(): lax.psum((mixed_part, recall_part.reshape(token_count, D)), 'narrow')  130 us
    reduce_scatter x1, waiting for transfers between devices, body(): lax.psum_scatter(grad_mem_out, 'wide', scatter_dimension=0, tiled=True)  92.6 us
    reduce_scatter x1, waiting for transfers between devices, body(): lax.psum_scatter(grad_down, 'wide', scatter_dimension=0, tiled=True)  91.9 us
    reduce_scatter x1, waiting for transfers between devices, body(): lax.psum_scatter(grad_mem_in, 'wide', scatter_dimension=0, tiled=True)  91.8 us
    psum x1, waiting for transfers between devices, body(): lax.psum(norm_back(grad_norm_mid, unit_mid, inverse_mid, gain_mid_f), 'na...  85.4 us
  transfers between devices with their start and end apart: 19, of which 15 were waited for; matrix products, arithmetic and copies ran while one was open for 17% of the time, Pallas kernels for 0%

commit v1 on v0

v1 whole, which is shorter than its diff:
```python
import jax
import jax.numpy as jnp
from jax import lax
from jax.sharding import PartitionSpec as P

D = 1024
HEADS = 16
HD = 64
LEN = 1024
CH = 512
WIN = 512
NP = 16
KC = 4


EPS = 1e-06
NEG = -1e30
STEP_IN = 128.0
STEP_OUT = 0.5
HIGHEST = lax.Precision.HIGHEST
LOW = jnp.bfloat16
F32 = jnp.float32


def segment_ids(lengths):
    doc_ends = jnp.cumsum(lengths)
    places = jnp.arange(LEN, dtype=jnp.int32)
    return jnp.sum((places[:, None] >= doc_ends[None, :]).astype(jnp.int32), axis=1)


def mix_inputs(projected, kernel, segment):
    feat_width = projected.shape[2]
    summed = kernel[:, 0][None] * projected
    for offset in range(1, KC):
        shifted = jnp.concatenate(
            [jnp.zeros((offset, 3, feat_width), projected.dtype), projected[:-offset]], 0
        )
        same_doc = jnp.concatenate(
            [jnp.zeros((offset,), jnp.bool_), segment[offset:] == segment[:-offset]], 0
        )
        summed = summed + kernel[:, offset][None] * jnp.where(same_doc[:, None, None], shifted, 0.0)
    active = jax.nn.silu(summed)
    paired = active[:, :2].reshape(LEN, 2, feat_width // HD, HD)
    paired = paired * lax.rsqrt(jnp.sum(paired * paired, -1, keepdims=True) + EPS)
    return jnp.concatenate([paired.reshape(LEN, 2, feat_width), active[:, 2:]], 1)


def product(formula, left_op, right_op):
    return jnp.einsum(formula, left_op, right_op, preferred_element_type=jnp.float32)


def norm_back(grad_norm, unit_val, inverse, gain_vec):
    scaled = grad_norm * gain_vec
    return inverse * (scaled - unit_val * jnp.mean(scaled * unit_val, -1, keepdims=True))


def swish_parts(pre_act):
    sig_val = jax.nn.sigmoid(pre_act)
    return (sig_val, sig_val * (1.0 + pre_act * (1.0 - sig_val)))


def flip(v, axis, bit):
    size = lax.axis_size(axis)
    return lax.ppermute(v, axis, [(i, i ^ bit) for i in range(size)])


def bits_of(axis):
    size = lax.axis_size(axis)
    out = []
    bit = 1
    while bit < size:
        out.append(bit)
        bit *= 2
    assert bit == size
    return out


def pick(v, index, axis=0):
    return lax.dynamic_index_in_dim(v, index, axis, keepdims=False)


def cut(v, start, width, axis):
    return lax.dynamic_slice_in_dim(v, start, width, axis)


def gather_cols(v, axis="narrow"):
    me = lax.axis_index(axis)
    parts = {0: v}
    for bit in reversed(bits_of(axis)):
        for key in list(parts):
            parts[key ^ bit] = flip(parts[key], axis, bit)
    stack = jnp.stack([parts[i] for i in range(len(parts))])
    return jnp.concatenate([pick(stack, i ^ me) for i in range(len(parts))], -1)


def sum_all(v, axis="narrow"):
    me = lax.axis_index(axis)
    bits = bits_of(axis)
    half = v.shape[0] // 2
    mine = me & 1
    low = v.astype(LOW)
    run = cut(low, mine * half, half, 0).astype(F32) + flip(
        cut(low, (1 - mine) * half, half, 0), axis, 1
    ).astype(F32)
    for bit in bits[1:]:
        low = run.astype(LOW)
        run = low.astype(F32) + flip(low, axis, bit).astype(F32)
    low = run.astype(LOW)
    other = flip(low, axis, 1)
    top = jnp.where(mine == 0, low, other)
    bottom = jnp.where(mine == 0, other, low)
    return jnp.concatenate([top, bottom], 0)


def scatter_cols(v, axis="narrow"):
    me = lax.axis_index(axis)
    size = lax.axis_size(axis)
    bits = bits_of(axis)
    width = v.shape[-1] // size
    low = v.astype(LOW)
    mine = me & 1

    def every_other(which):
        return jnp.concatenate(
            [cut(low, (2 * i + which) * width, width, 1) for i in range(size // 2)], 1
        )

    run = every_other(mine).astype(F32) + flip(every_other(1 - mine), axis, 1).astype(F32)
    for bit in reversed(bits[1:]):
        half = run.shape[1] // 2
        mine = (me // bit) & 1
        send = cut(run, (1 - mine) * half, half, 1).astype(LOW)
        run = cut(run, mine * half, half, 1) + flip(send, axis, bit).astype(F32)
    return run


def scatter_rows(v, axis="wide"):
    me = lax.axis_index(axis)
    size = lax.axis_size(axis)
    tail = v.shape[1:]
    run = v.astype(LOW).reshape((size, v.shape[0] // size) + tail)
    for bit in bits_of(axis):
        mine = (me // bit) & 1
        run = run.reshape((run.shape[0] // 2, 2) + run.shape[1:])
        send = pick(run, 1 - mine, 1).astype(LOW)
        run = pick(run, mine, 1).astype(F32) + flip(send, axis, bit).astype(F32)
    return run[0]


def sum_small(v, axes):
    for axis in axes:
        for bit in bits_of(axis):
            v = v + flip(v, axis, bit)
    return v


def window_mask(segments, block_start):
    places = jnp.arange(LEN, dtype=jnp.int32)
    query_pos = block_start + jnp.arange(CH, dtype=jnp.int32)
    query_seg = segments[block_start : block_start + CH]
    return (
        (places[None, :] <= query_pos[:, None])
        & (query_pos[:, None] - places[None, :] < WIN)
        & (segments[None, :] == query_seg[:, None])
    )


def body(
    tokens,
    gain_in,
    gain_mid,
    w_qkv,
    w_gate,
    w_decay,
    conv_kernel,
    persistent,
    w_out,
    mem_in,
    mem_out,
    w_up,
    w_down,
    doc_len,
    reset,
    cotangent,
):
    assert doc_len.shape[0] == 1
    width = w_qkv.shape[2]
    heads = width // HD
    ffn = w_up.shape[2]
    lead = lax.axis_index("narrow") * width
    score_scale = HD**0.5
    segment = segment_ids(doc_len[0])
    keep = 1.0 - reset.astype(F32)[0]
    gain_in_f = gain_in.astype(F32)
    gain_mid_f = gain_mid.astype(F32)
    mem_in_f = mem_in.astype(F32)
    mem_out_f = mem_out.astype(F32)
    inputs = tokens.astype(F32)
    inverse_in = lax.rsqrt(jnp.mean(inputs * inputs, -1, keepdims=True) + EPS)
    unit_in = inputs * inverse_in
    normed_in = (unit_in * gain_in_f).astype(LOW)
    w_qkv_t = w_qkv.transpose(1, 0, 2)
    projected = product("td,cdf->tcf", normed_in, w_qkv_t)

    def mixing(proj_in, kernel):
        return mix_inputs(proj_in, kernel, segment)

    mixed_act, mixing_back = jax.vjp(mixing, projected, conv_kernel.astype(F32))
    act_low = mixed_act.astype(LOW)
    query_loc, key_loc, value_loc = act_low[:, 0], act_low[:, 1], act_low[:, 2]
    key_value = gather_cols(jnp.stack([key_loc[:CH], value_loc[:CH]]))
    key_block, value_block = key_value[0], key_value[1]
    query_all = gather_cols(query_loc)
    cot_full = gather_cols(cotangent)
    mem_gates = jax.nn.sigmoid(product("td,dc->tc", normed_in, w_decay))
    decay_row = jnp.mean(mem_gates[:CH, 0])
    step_rate = jnp.mean(mem_gates[:CH, 1])
    gate_act = jax.nn.sigmoid(product("td,dh->th", normed_in, w_gate))
    gate_wide = jnp.repeat(gate_act, HD, axis=1)
    key_pre = product("cd,df->cf", key_block, mem_in)
    key_sig, key_slope = swish_parts(key_pre)
    key_hidden = (key_pre * key_sig).astype(LOW)
    predicted = sum_all(product("cf,fd->cd", key_hidden, mem_out)).astype(F32)
    first_pre = product("cd,df->cf", query_all[:CH], mem_in)
    first_sig, first_slope = swish_parts(first_pre)
    first_hidden = (first_pre * first_sig).astype(LOW)
    first_recall = product("cf,fd->cd", first_hidden, mem_out)
    query_h = query_loc.reshape(LEN, heads, HD)
    key_h = key_loc.reshape(LEN, heads, HD)
    value_h = value_loc.reshape(LEN, heads, HD)
    pers_keys = persistent[0].reshape(NP, heads, HD)
    pers_values = persistent[1].reshape(NP, heads, HD)

    def block_scores(start):
        query_blk = query_h[start : start + CH]
        allowed = window_mask(segment, start)[None]
        scores = jnp.where(allowed, score_scale * product("qhd,khd->hqk", query_blk, key_h), NEG)
        pers_scores = score_scale * product("qhd,khd->hqk", query_blk, pers_keys)
        return (query_blk, scores, pers_scores)

    peak_list = []
    normal_list = []
    mixed_list = []
    att_list = []
    for start in range(0, LEN, CH):
        query_blk, scores, pers_scores = block_scores(start)
        row_peak = jnp.maximum(jnp.max(scores, -1), jnp.max(pers_scores, -1))[..., None]
        weights = jnp.exp(scores - row_peak)
        pers_weights = jnp.exp(pers_scores - row_peak)
        normal = jnp.sum(weights, -1, keepdims=True) + jnp.sum(pers_weights, -1, keepdims=True)
        prob_low = (weights / normal).astype(LOW)
        pers_low = (pers_weights / normal).astype(LOW)
        att = product("hqk,khd->qhd", prob_low, value_h) + product(
            "hqk,khd->qhd", pers_low, pers_values
        )
        att = att.reshape(CH, width).astype(LOW)
        att_list.append(att)
        mixed_list.append(product("td,df->tf", att, w_out))
        peak_list.append(row_peak)
        normal_list.append(normal)
    attended = jnp.concatenate(att_list, 0)
    joined_first = sum_all(mixed_list[0] + gate_wide[:CH] * first_recall)
    error_low = (predicted - value_block.astype(F32)).astype(LOW)
    back_hidden = product("cd,fd->cf", error_low, mem_out)
    slope_low = (back_hidden * key_slope).astype(LOW)
    grad_in = product("cd,cf->df", key_block, slope_low) / CH
    grad_out = product("cf,cd->fd", key_hidden, error_low) / CH
    memory_in = mem_in_f - keep * (decay_row * mem_in_f + step_rate * STEP_IN * grad_in)
    memory_out = mem_out_f - keep * (decay_row * mem_out_f + step_rate * STEP_OUT * grad_out)
    memory_in_low = memory_in.astype(LOW)
    memory_out_low = memory_out.astype(LOW)
    second_pre = product("cd,df->cf", query_all[CH:], memory_in_low)
    second_sig, second_slope = swish_parts(second_pre)
    second_hidden = (second_pre * second_sig).astype(LOW)
    second_recall = product("cf,fd->cd", second_hidden, memory_out_low)
    joined_second = sum_all(mixed_list[1] + gate_wide[CH:] * second_recall)

    w_gate_up = w_up.transpose(1, 0, 2)

    def feed(part, joined):
        rows = slice(part * CH, part * CH + CH)
        middle = inputs[rows] + joined.astype(F32)
        inverse = lax.rsqrt(jnp.mean(middle * middle, -1, keepdims=True) + EPS)
        unit = middle * inverse
        normed = (unit * gain_mid_f).astype(LOW)
        gate_val = product("td,df->tf", normed, w_gate_up[0])
        up_val = product("td,df->tf", normed, w_gate_up[1])
        sig = jax.nn.sigmoid(gate_val)
        hidden = (gate_val * sig * up_val).astype(LOW)
        ffn_out = scatter_cols(product("tf,fd->td", hidden, w_down))
        output = (cut(middle, lead, width, 1) + ffn_out).astype(LOW)
        cot = cot_full[rows]
        grad_hidden = product("td,fd->tf", cot, w_down)
        grad_gate = (grad_hidden * up_val * sig * (1.0 + gate_val * (1.0 - sig))).astype(LOW)
        grad_up = (grad_hidden * gate_val * sig).astype(LOW)
        grad_norm = product("tf,df->td", grad_gate, w_gate_up[0]) + product(
            "tf,df->td", grad_up, w_gate_up[1]
        )
        gain_part = jnp.sum(grad_norm * unit, 0)
        summed = sum_all(norm_back(grad_norm, unit, inverse, gain_mid_f))
        grad_middle = summed.astype(F32) + cot.astype(F32)
        return output, normed, hidden, grad_gate, grad_up, gain_part, grad_middle

    out_a, norm_a, hid_a, gg_a, gu_a, gain_a, grad_mid_a = feed(0, joined_first)
    out_b, norm_b, hid_b, gg_b, gu_b, gain_b, grad_mid_b = feed(1, joined_second)
    output = jnp.concatenate([out_a, out_b], 0)
    gain_mid_part = gain_a + gain_b
    normed_mid = jnp.concatenate([norm_a, norm_b], 0)
    hidden = jnp.concatenate([hid_a, hid_b], 0)
    grad_down = scatter_rows(product("td,tf->df", cot_full, hidden))
    grad_up_gate = scatter_rows(
        product("td,tf->df", normed_mid, jnp.concatenate([gg_a, gg_b], 0))
    )
    grad_up_up = scatter_rows(product("td,tf->df", normed_mid, jnp.concatenate([gu_a, gu_b], 0)))
    grad_middle = jnp.concatenate([grad_mid_a, grad_mid_b], 0)

    def gate_terms(recall, grad_mid, gates):
        terms = jnp.sum((recall * grad_mid).reshape(CH, HEADS, HD), -1)
        return terms * gates * (1.0 - gates)

    second_grad = (gate_wide[CH:] * grad_mid_b).astype(LOW)
    grad_memory_out = product("cf,cd->fd", second_hidden, second_grad)
    grad_second_pre = (product("cd,fd->cf", second_grad, memory_out_low) * second_slope).astype(LOW)
    grad_memory_in = product("cd,cf->df", query_all[CH:], grad_second_pre)
    grad_query_second = product("cf,df->cd", grad_second_pre, memory_in_low)
    factor = -(keep * step_rate)
    grad_gin = (factor * STEP_IN * grad_memory_in).astype(LOW)
    grad_gout = (factor * STEP_OUT * grad_memory_out).astype(LOW)
    grad_slope = product("cd,df->cf", key_block, grad_gin) / CH
    grad_error = product("cf,fd->cd", key_hidden, grad_gout) / CH
    grad_back_low = (grad_slope * key_slope).astype(LOW)
    grad_error = grad_error + product("cf,fd->cd", grad_back_low, mem_out)
    grad_pred_low = sum_all(grad_error)
    grad_key_block = product("cf,df->cd", slope_low, grad_gin) / CH
    grad_key_hidden = product("cd,fd->cf", error_low, grad_gout) / CH
    first_grad = (gate_wide[:CH] * grad_mid_a).astype(LOW)
    grad_mem_out = product("cf,cd->fd", first_hidden, first_grad)
    grad_first_pre = (product("cd,fd->cf", first_grad, mem_out) * first_slope).astype(LOW)
    grad_mem_in = product("cd,cf->df", query_all[:CH], grad_first_pre)
    grad_query_first = product("cf,df->cd", grad_first_pre, mem_in)
    query_share = scatter_cols(jnp.concatenate([grad_query_first, grad_query_second], 0))
    grad_head_gate = jnp.concatenate(
        [
            gate_terms(first_recall, grad_mid_a, gate_act[:CH]),
            gate_terms(second_recall, grad_mid_b, gate_act[CH:]),
        ],
        0,
    )
    head_gate_low = grad_head_gate.astype(LOW)
    grad_gate_w = product("td,th->hd", normed_in, head_gate_low)
    grad_mixed_low = grad_middle.astype(LOW)
    grad_out_w = scatter_rows(product("td,tf->df", grad_mixed_low, attended))
    grad_att = product("td,fd->tf", grad_mixed_low, w_out).astype(LOW).reshape(LEN, heads, HD)
    grad_query_list = []
    grad_key_att = 0.0
    grad_value_att = 0.0
    grad_pers_key = 0.0
    grad_pers_value = 0.0
    for index, start in enumerate(range(0, LEN, CH)):
        query_blk, scores, pers_scores = block_scores(start)
        prob_full = jnp.exp(scores - peak_list[index]) / normal_list[index]
        pers_probs = jnp.exp(pers_scores - peak_list[index]) / normal_list[index]
        grad_blk = grad_att[start : start + CH]
        grad_probs = product("qhd,khd->hqk", grad_blk, value_h)
        grad_pers_probs = product("qhd,khd->hqk", grad_blk, pers_values)
        center = jnp.sum(prob_full * grad_probs, -1, keepdims=True) + jnp.sum(
            pers_probs * grad_pers_probs, -1, keepdims=True
        )
        grad_scores = (prob_full * (grad_probs - center)).astype(LOW)
        grad_pers_scores = (pers_probs * (grad_pers_probs - center)).astype(LOW)
        grad_query_list.append(
            score_scale
            * (
                product("hqk,khd->qhd", grad_scores, key_h)
                + product("hqk,khd->qhd", grad_pers_scores, pers_keys)
            )
        )
        grad_key_att = grad_key_att + score_scale * product("hqk,qhd->khd", grad_scores, query_blk)
        grad_value_att = grad_value_att + product("hqk,qhd->khd", prob_full.astype(LOW), grad_blk)
        grad_pers_key = grad_pers_key + score_scale * product(
            "hqk,qhd->khd", grad_pers_scores, query_blk
        )
        grad_pers_value = grad_pers_value + product("hqk,qhd->khd", pers_probs.astype(LOW), grad_blk)
    grad_query_att = jnp.concatenate(grad_query_list, 0).reshape(LEN, width)
    grad_key_att = grad_key_att.reshape(LEN, width)
    grad_value_att = grad_value_att.reshape(LEN, width)
    grad_pred = grad_pred_low.astype(F32)
    grad_key_hidden = grad_key_hidden + product("cd,fd->cf", grad_pred_low, mem_out)
    key_curve = key_sig * (1.0 - key_sig) * (2.0 + key_pre * (1.0 - 2.0 * key_sig))
    grad_key_pre = (grad_key_hidden * key_slope + grad_slope * back_hidden * key_curve).astype(LOW)
    grad_key_block = grad_key_block + product("cf,df->cd", grad_key_pre, mem_in)
    key_share = scatter_cols(grad_key_block)
    retain = 1.0 - keep * decay_row
    grad_mem_in = (
        grad_mem_in + retain * grad_memory_in + product("cd,cf->df", key_block, grad_key_pre)
    )
    grad_mem_out = (
        grad_mem_out
        + retain * grad_memory_out
        + product("cf,cd->fd", grad_back_low, error_low)
        + product("cf,cd->fd", key_hidden, grad_pred_low)
    )
    in_shard = scatter_rows(grad_mem_in)
    back_shard = scatter_rows(grad_mem_out.T)
    decay_part = -keep * (jnp.sum(mem_in_f * grad_memory_in) + jnp.sum(mem_out_f * grad_memory_out))
    step_part = -keep * (
        STEP_IN * jnp.sum(grad_in * grad_memory_in) + STEP_OUT * jnp.sum(grad_out * grad_memory_out)
    )
    value_share = -cut(grad_pred, lead, width, 1)
    tail_zeros = jnp.zeros((LEN - CH, width), F32)
    grad_act = jnp.stack(
        [
            grad_query_att + query_share,
            grad_key_att + jnp.concatenate([key_share, tail_zeros], 0),
            grad_value_att + jnp.concatenate([value_share, tail_zeros], 0),
        ],
        1,
    )
    grad_proj, grad_conv = mixing_back(grad_act)
    grad_proj_low = grad_proj.astype(LOW)
    grad_norm_part = product("tcf,cdf->td", grad_proj_low, w_qkv_t) + product(
        "th,dh->td", head_gate_low, w_gate
    )
    gate_slopes = mem_gates * (1.0 - mem_gates)
    in_first = (jnp.arange(LEN) < CH).astype(F32) / CH
    step_logit = step_part * gate_slopes[:, 1] * in_first
    decay_logit = decay_part * gate_slopes[:, 0] * in_first
    decay_w = w_decay.astype(F32)
    grad_norm_part = (
        grad_norm_part
        + step_logit[:, None] * decay_w[:, 1][None]
        + decay_logit[:, None] * decay_w[:, 0][None]
    )
    normed_f = normed_in.astype(F32)
    step_w = jnp.sum(normed_f * step_logit[:, None], 0)
    decay_w_part = jnp.sum(normed_f * decay_logit[:, None], 0)
    gain_in_part = jnp.sum(grad_norm_part * unit_in, 0)
    input_share = scatter_cols(norm_back(grad_norm_part, unit_in, inverse_in, gain_in_f))
    grad_input = input_share + cut(grad_middle, lead, width, 1)
    grad_qkv_w = [
        scatter_rows(product("td,tf->df", normed_in, grad_proj_low[:, i])) for i in range(3)
    ]
    pers_part = jnp.concatenate(
        [grad_pers_key.reshape(NP, width), grad_pers_value.reshape(NP, width)], 0
    )
    own_part = jnp.concatenate([grad_conv.reshape(3 * KC, width), pers_part], 0)
    own_all = gather_cols(sum_small(own_part, ("wide",)))
    vec_part = jnp.concatenate(
        [jnp.stack([gain_in_part, gain_mid_part, decay_w_part, step_w]), grad_gate_w], 0
    )
    vec_all = sum_small(vec_part, ("narrow", "wide"))
    conv_sum = own_all[: 3 * KC].reshape(3, KC, D)
    pers_sum = own_all[3 * KC :].reshape(2, NP, D)
    gate_rows = D // lax.axis_size("wide")
    gate_shard = cut(vec_all[4:], lax.axis_index("wide") * gate_rows, gate_rows, 1).T
    return (
        output,
        grad_input,
        vec_all[0],
        vec_all[1],
        jnp.stack(grad_qkv_w, 1),
        gate_shard,
        vec_all[2:4].T,
        conv_sum,
        pers_sum,
        grad_out_w.T,
        in_shard,
        back_shard.T,
        jnp.stack([grad_up_gate, grad_up_up], 1),
        grad_down.T,
    )


def solution(mesh):
    in_specs = (
        P("wide", None),
        P(),
        P(),
        P(None, None, "narrow"),
        P(),
        P(),
        P(None, None, "narrow"),
        P(None, None, "narrow"),
        P("narrow", None),
        P(None, "narrow"),
        P("narrow", None),
        P(None, None, "narrow"),
        P("narrow", None),
        P("wide", None),
        P("wide"),
        P("wide", "narrow"),
    )
    out_specs = (
        P("wide", "narrow"),
        P("wide", "narrow"),
        P(),
        P(),
        P("wide", None, "narrow"),
        P("wide", None),
        P(),
        P(),
        P(),
        P("narrow", "wide"),
        P("wide", "narrow"),
        P("narrow", "wide"),
        P("wide", None, "narrow"),
        P("narrow", "wide"),
    )
    return jax.shard_map(body, mesh=mesh, in_specs=in_specs, out_specs=out_specs, check_vma=False)
```

time: 1570 us -> 659 us (0.42)
  waiting for transfers between devices: 1120 us -> 175 us
  starting transfers between devices: 1.97 us -> 67 us
  matrix products: 200 us -> 174 us
    reduce_scatter x11 -> x0, waiting for transfers between devices: 595 us -> none  [the longest x1 149 us: body(): lax.psum_scatter(grad_up_w, 'wide', scatter_dimension=0, tiled=True)]
    psum x6 -> x0, waiting for transfers between devices: 499 us -> none  [the longest x2 204 us: body(): lax.psum((gain_in_part, gain_mid_part, step_w, decay_w_part, conv_full, p...]
    ppermute x0 -> x75, waiting for transfers between devices: none -> 175 us  [flip(): return lax.ppermute(v, axis, [(i, i ^ bit) for i in range(size)])]
    ppermute x0 -> x75, starting transfers between devices: none -> 67 us  [flip(): return lax.ppermute(v, axis, [(i, i ^ bit) for i in range(size)])]
    dot_general x10 -> x0, matrix products: 33.8 us -> none  [the longest x1 6.97 us: body(): jnp.dot(normed_mid, w_up.reshape(D, 2 * ffn_width), preferred_element_typ...]
    all_gather x2 -> x0, waiting for transfers between devices: 28.2 us -> none  [the longest x1 18.9 us: body(): full_act = lax.all_gather(act_low, 'narrow', axis=3, tiled=True)]
    dynamic_slice x0 -> x16, local copies, waits for them, and re-layouts: none -> 22.3 us  [the longest x6 15.8 us: pick(): return lax.dynamic_index_in_dim(v, index, axis, keepdims=False)]
    mul x5 -> x1, other arithmetic: 18.3 us -> 0.01 us  [body(): step_logit = step_part * gate_slopes[:, 1] * in_first]
  transfers between devices with their start and end apart: 19 -> 75, of which waited for: 15 -> 25; matrix products, arithmetic and copies ran while one was open for 17% -> 55% of each run, Pallas kernels for 0% -> 0%
where the time goes in v1:
time: 659 us; the launch traced here: 648 us
  waiting for transfers between devices  175 us (27%)
  matrix products  174 us (26%)
  local copies, waits for them, and re-layouts  111 us (17%)
  other arithmetic  111 us (17%)
  starting transfers between devices  67 us (10%)
  between operations  9.95 us (2%)
    ppermute x75, waiting for transfers between devices, flip(): return lax.ppermute(v, axis, [(i, i ^ bit) for i in range(size)])  175 us
    dot_general x79, matrix products, product(): jnp.einsum(formula, left_op, right_op, preferred_element_type=jnp.float32)  174 us
    ppermute x75, starting transfers between devices, flip(): return lax.ppermute(v, axis, [(i, i ^ bit) for i in range(size)])  67 us
    unnamed x390, local copies, waits for them, and re-layouts  48.7 us
    dynamic_slice x6, local copies, waits for them, and re-layouts, pick(): return lax.dynamic_index_in_dim(v, index, axis, keepdims=False)  15.8 us
    add x18, other arithmetic, scatter_rows(): run = pick(run, mine, 1).astype(F32) + flip(send, axis, bit).astype(F32)  15.7 us
  transfers between devices with their start and end apart: 75, of which 25 were waited for; matrix products, arithmetic and copies ran while one was open for 55% of the time, Pallas kernels for 0%

profile of v1, /device:TPU:0, one launch (start us, length us, event | category | flops | bytes accessed | tf_op | source)
XLA Modules:
  0.0 648.1 jit_solution(13777657501037320165)
XLA Ops:
  6.5 4.0 copy.192
  16.2 4.9 fusion.201
  41.7 3.6 fusion.97
  45.3 3.5 fusion.94
  69.1 12.5 %collective-permute-done.12 = bf16[256,1024]{0,1:T(8,128)(2,1)S(1)} collective-permute-done((bf16[256,1024]{0,1:T(8,128)(2,1)S(1)}, bf16[256,1024]{0,1:T(8,128)(2,1)S(1)}, u32[]{:S(2)}, u32[]{:S(2)}) %collective-permute-start.12) | collective-permute-done | bytes 524320 | tf_op jit(solution)/shard_map/ppermute | solution.py:64
  88.7 3.6 fusion.11
  93.7 3.4 fusion.15
  102.1 4.1 convert_element_type.650
  106.2 5.5 copy.371
  119.3 9.5 %collective-permute-done.4 = bf16[256,1024]{0,1:T(8,128)(2,1)S(1)} collective-permute-done((bf16[256,1024]{0,1:T(8,128)(2,1)S(1)}, bf16[256,1024]{0,1:T(8,128)(2,1)S(1)}, u32[]{:S(2)}, u32[]{:S(2)}) %collective-permute-start.4) | collective-permute-done | bytes 524320 | tf_op jit(solution)/shard_map/ppermute | solution.py:64
  129.0 10.3 %collective-permute-done.15 = bf16[256,1024]{0,1:T(8,128)(2,1)S(1)} collective-permute-done((bf16[256,1024]{0,1:T(8,128)(2,1)S(1)}, bf16[256,1024]{0,1:T(8,128)(2,1)S(1)}, u32[]{:S(2)}, u32[]{:S(2)}) %collective-permute-start.15) | collective-permute-done | bytes 524320 | tf_op jit(solution)/shard_map/ppermute | solution.py:64
  196.7 6.0 collective-permute-done.18
  203.4 4.9 collective-permute-done.7
  210.0 9.6 %collective-permute-done.26 = bf16[256,1024]{0,1:T(8,128)(2,1)} collective-permute-done((bf16[256,1024]{0,1:T(8,128)(2,1)S(1)}, bf16[256,1024]{0,1:T(8,128)(2,1)}, u32[]{:S(2)}, u32[]{:S(2)}) %collective-permute-start.26) | collective-permute-done | bytes 524320 | tf_op jit(solution)/shard_map/ppermute | solution.py:64
  220.9 8.6 %collective-permute-done.23 = bf16[256,1024]{0,1:T(8,128)(2,1)} collective-permute-done((bf16[256,1024]{0,1:T(8,128)(2,1)}, bf16[256,1024]{0,1:T(8,128)(2,1)}, u32[]{:S(2)}, u32[]{:S(2)}) %collective-permute-start.23) | collective-permute-done | bytes 524320 | tf_op jit(solution)/shard_map/ppermute | solution.py:64
  238.5 16.4 %collective-permute-done.69 = bf16[4,128,1024]{2,1,0:T(8,128)(2,1)} collective-permute-done((bf16[4,128,1024]{2,1,0:T(8,128)(2,1)}, bf16[4,128,1024]{2,1,0:T(8,128)(2,1)}, u32[]{:S(2)}, u32[]{:S(2)}) %collective-permute-start.69) | collective-permute-done | bytes 1048608 | tf_op jit(solution)/shard_map/ppermute | solution.py:64
  269.9 3.3 fusion.190
  279.6 3.6 fusion.57
  284.9 3.6 fusion.192
  290.7 3.9 multiply_reduce_fusion.5
  294.6 5.5 copy.271
  300.1 6.0 multiply_convert_fusion.7
  308.8 3.3 fusion.217
  315.8 5.6 multiply_reduce_fusion.1
  321.4 5.4 multiply_convert_fusion.1
  330.1 5.6 multiply_reduce_fusion
  341.2 6.5 %fusion.80 = f32[4,64,1024]{2,1,0:T(8,128)} fusion(f32[4,64,1024]{2,1,0:T(8,128)} %fusion.57, bf16[512,4,64]{0,2,1:T(8,128)(2,1)S(1)} %bitcast.589, f32[4,512,1024]{2,1,0:T(8,128)} %copy-done.7, f32[4,512]{1,0:T(4,128)S(1)} %add.671, f32[4,512]{1,0:T(4,128)S(1)} %max.14, pred[512,1024]{1,0:T(8,128)(4,1)S(1)} %copy-done.37), kind=kOutput, calls=%fused_computation.204 | convolution fusion | flops 279183360 | bytes 11288576 | tf_op jit(solution)/shard_map/hqk,qhd->khd/dot_general | solution.py:49
  350.0 5.4 copy.261
  355.4 5.3 fusion.127
  360.7 4.0 add_convert_fusion.3
  370.0 7.6 %multiply_convert_fusion = bf16[4,512,1024]{2,1,0:T(8,128)(2,1)S(1)} fusion(f32[4,512,1024]{2,1,0:T(8,128)} %get-tuple-element.203, f32[4,512]{1,0:T(4,128)S(1)} %add.738, f32[4,512]{1,0:T(4,128)S(1)} %copy-done.142, f32[4,512]{1,0:T(4,128)S(1)} %copy-done.132, f32[4,512,1024]{2,1,0:T(8,128)} %copy-done.6, pred[512,1024]{1,0:T(8,128)(4,1)S(1)} %copy-done.35), kind=kLoop, calls=%fused_computation | loop fusion | flops 14680064 | bytes 21520384 | tf_op jit(solution)/shard_map/convert_element_type | solution.py:369
  398.3 17.6 %collective-permute-done.74 = bf16[1,128,1024]{2,1,0:T(8,128)(2,1)S(1)} collective-permute-done((bf16[1,128,1024]{2,1,0:T(8,128)(2,1)S(1)}, bf16[1,128,1024]{2,1,0:T(8,128)(2,1)S(1)}, u32[]{:S(2)}, u32[]{:S(2)}) %collective-permute-start.74) | collective-permute-done | bytes 262176 | tf_op jit(solution)/shard_map/ppermute | solution.py:64
  416.8 4.8 collective-permute-done.68
  430.8 5.1 collective-permute-done.29
  444.1 4.4 fusion.33
  457.5 4.7 reshape_reshape.31
  465.3 6.0 fusion.19
  474.4 6.3 constant_dynamic-slice_fusion.1
  480.8 5.8 copy.335
  486.6 5.8 copy.336
  498.6 6.4 collective-permute-done.34
  508.8 4.8 multiply_reduce_fusion.10
  524.6 6.1 multiply_reduce_fusion.2
  553.8 11.2 %collective-permute-done.39 = f32[20,1024]{1,0:T(8,128)S(1)} collective-permute-done((f32[20,1024]{1,0:T(8,128)S(1)}, f32[20,1024]{1,0:T(8,128)S(1)}, u32[]{:S(2)}, u32[]{:S(2)}) %collective-permute-start.39) | collective-permute-done | bytes 81952 | tf_op jit(solution)/shard_map/ppermute | solution.py:64
  577.5 22.3 %collective-permute-done.49 = bf16[2,128,256]{2,1,0:T(8,128)(2,1)S(1)} collective-permute-done((bf16[2,128,256]{2,1,0:T(8,128)(2,1)S(1)}, bf16[2,128,256]{2,1,0:T(8,128)(2,1)S(1)}, u32[]{:S(2)}, u32[]{:S(2)}) %collective-permute-start.49) | collective-permute-done | bytes 131104 | tf_op jit(solution)/shard_map/ppermute | solution.py:64
  608.9 3.5 collective-permute-done.41
  620.0 3.5 collective-permute-start.65
  628.0 10.3 %collective-permute-done.65 = bf16[1,128,1024]{2,1,0:T(8,128)(2,1)S(1)} collective-permute-done((bf16[1,128,1024]{2,1,0:T(8,128)(2,1)S(1)}, bf16[1,128,1024]{2,1,0:T(8,128)(2,1)S(1)}, u32[]{:S(2)}, u32[]{:S(2)}) %collective-permute-start.65) | collective-permute-done | bytes 262176 | tf_op jit(solution)/shard_map/ppermute | solution.py:64
  (804 shorter events, 324.3 us)
Async XLA Ops:
  0.7 111.7 %collective-permute-start.20 = (bf16[1024,256]{1,0:T(8,128)(2,1)}, bf16[1024,256]{1,0:T(8,128)(2,1)}, u32[]{:S(2)}, u32[]{:S(2)}) collective-permute-start(bf16[1024,256]{1,0:T(8,128)(2,1)} %param.31), channel_id=1, source_target_pairs={{0,2},{1,3},{2,0},{3,1},{4,6},{5,7},{6,4},{7,5},{8,10},{9,11},{10,... | collective-permute-start | bytes 1572872 | tf_op jit(solution)/shard_map/ppermute | solution.py:64
  3.7 114.2 %collective-permute-start.19 = (bf16[1024,256]{1,0:T(8,128)(2,1)}, bf16[1024,256]{1,0:T(8,128)(2,1)}, u32[]{:S(2)}, u32[]{:S(2)}) collective-permute-start(bf16[1024,256]{1,0:T(8,128)(2,1)} %param.31), channel_id=1, source_target_pairs={{0,1},{1,0},{2,3},{3,2},{4,5},{5,4},{6,7},{7,6},{8,9},{9,8},{10,11... | collective-permute-start | bytes 1572872 | tf_op jit(solution)/shard_map/ppermute | solution.py:64
  24.5 33.6 %collective-permute-start.8 = (bf16[2,512,256]{1,2,0:T(8,128)(2,1)}, bf16[2,512,256]{1,2,0:T(8,128)(2,1)}, u32[]{:S(2)}, u32[]{:S(2)}) collective-permute-start(bf16[2,512,256]{1,2,0:T(8,128)(2,1)} %get-tuple-element.153), channel_id=1, source_target_pairs={{0,1},{1,0},{2,3},{3,2},{4,5},{5,4},{6,7},{7,6},{8,9},{9,8},{10,11... | collective-permute-start | bytes 1572872 | tf_op jit(solution)/shard_map/ppermute | solution.py:64
  25.0 29.0 %collective-permute-start.9 = (bf16[2,512,256]{1,2,0:T(8,128)(2,1)}, bf16[2,512,256]{1,2,0:T(8,128)(2,1)}, u32[]{:S(2)}, u32[]{:S(2)}) collective-permute-start(bf16[2,512,256]{1,2,0:T(8,128)(2,1)} %get-tuple-element.153), channel_id=1, source_target_pairs={{0,2},{1,3},{2,0},{3,1},{4,6},{5,7},{6,4},{7,5},{8,10},{9,11},{10,... | collective-permute-start | bytes 1572872 | tf_op jit(solution)/shard_map/ppermute | solution.py:64
  26.2 31.3 %collective-permute-start.1 = (bf16[1024,256]{0,1:T(8,128)(2,1)}, bf16[1024,256]{0,1:T(8,128)(2,1)}, u32[]{:S(2)}, u32[]{:S(2)}) collective-permute-start(bf16[1024,256]{0,1:T(8,128)(2,1)} %get-tuple-element.146), channel_id=1, source_target_pairs={{0,2},{1,3},{2,0},{3,1},{4,6},{5,7},{6,4},{7,5},{8,10},{9,11},{10,... | collective-permute-start | bytes 1572872 | tf_op jit(solution)/shard_map/ppermute | solution.py:64
  67.4 14.3 %collective-permute-start.12 = (bf16[256,1024]{0,1:T(8,128)(2,1)S(1)}, bf16[256,1024]{0,1:T(8,128)(2,1)S(1)}, u32[]{:S(2)}, u32[]{:S(2)}) collective-permute-start(bf16[256,1024]{0,1:T(8,128)(2,1)S(1)} %add_convert_fusion.13), channel_id=1, source_target_pairs={{0,2},{1,3},{2,0},{3,1},{4,6},{5,7},{6,4},{7,5},{8,10},{9,11},{10,... | collective-permute-start | bytes 1572872 | tf_op jit(solution)/shard_map/ppermute | solution.py:64
  84.8 27.8 %collective-permute-start.3 = (bf16[256,1024]{0,1:T(8,128)(2,1)}, bf16[256,1024]{0,1:T(8,128)(2,1)}, u32[]{:S(2)}, u32[]{:S(2)}) collective-permute-start(bf16[256,1024]{0,1:T(8,128)(2,1)} %constant_dynamic-slice_fusion.28), channel_id=1, source_target_pairs={{0,1},{1,0},{2,3},{3,2},{4,5},{5,4},{6,7},{7,6},{8,9},{9,8},{10,11... | collective-permute-start | bytes 1572872 | tf_op jit(solution)/shard_map/ppermute | solution.py:64
  100.0 14.3 %collective-permute-start.14 = (bf16[256,1024]{0,1:T(8,128)(2,1)}, bf16[256,1024]{0,1:T(8,128)(2,1)S(1)}, u32[]{:S(2)}, u32[]{:S(2)}) collective-permute-start(bf16[256,1024]{0,1:T(8,128)(2,1)} %constant_dynamic-slice_fusion.22), channel_id=1, source_target_pairs={{0,1},{1,0},{2,3},{3,2},{4,5},{5,4},{6,7},{7,6},{8,9},{9,8},{10,11... | collective-permute-start | bytes 1572872 | tf_op jit(solution)/shard_map/ppermute | solution.py:64
  114.0 14.8 %collective-permute-start.4 = (bf16[256,1024]{0,1:T(8,128)(2,1)S(1)}, bf16[256,1024]{0,1:T(8,128)(2,1)S(1)}, u32[]{:S(2)}, u32[]{:S(2)}) collective-permute-start(bf16[256,1024]{0,1:T(8,128)(2,1)S(1)} %add_convert_fusion.15), channel_id=1, source_target_pairs={{0,2},{1,3},{2,0},{3,1},{4,6},{5,7},{6,4},{7,5},{8,10},{9,11},{10,... | collective-permute-start | bytes 1572872 | tf_op jit(solution)/shard_map/ppermute | solution.py:64
  115.5 23.8 %collective-permute-start.15 = (bf16[256,1024]{0,1:T(8,128)(2,1)S(1)}, bf16[256,1024]{0,1:T(8,128)(2,1)S(1)}, u32[]{:S(2)}, u32[]{:S(2)}) collective-permute-start(bf16[256,1024]{0,1:T(8,128)(2,1)S(1)} %add_convert_fusion.11), channel_id=1, source_target_pairs={{0,2},{1,3},{2,0},{3,1},{4,6},{5,7},{6,4},{7,5},{8,10},{9,11},{10,... | collective-permute-start | bytes 1572872 | tf_op jit(solution)/shard_map/ppermute | solution.py:64
  128.9 22.6 %collective-permute-start.5 = (bf16[256,1024]{0,1:T(8,128)(2,1)S(1)}, bf16[256,1024]{0,1:T(8,128)(2,1)}, u32[]{:S(2)}, u32[]{:S(2)}) collective-permute-start(bf16[256,1024]{0,1:T(8,128)(2,1)S(1)} %add_convert_fusion.14), channel_id=1, source_target_pairs={{0,1},{1,0},{2,3},{3,2},{4,5},{5,4},{6,7},{7,6},{8,9},{9,8},{10,11... | collective-permute-start | bytes 1572872 | tf_op jit(solution)/shard_map/ppermute | solution.py:64
  140.3 12.9 %collective-permute-start.16 = (bf16[256,1024]{0,1:T(8,128)(2,1)}, bf16[256,1024]{0,1:T(8,128)(2,1)}, u32[]{:S(2)}, u32[]{:S(2)}) collective-permute-start(bf16[256,1024]{0,1:T(8,128)(2,1)} %add_convert_fusion.10), channel_id=1, source_target_pairs={{0,1},{1,0},{2,3},{3,2},{4,5},{5,4},{6,7},{7,6},{8,9},{9,8},{10,11... | collective-permute-start | bytes 1572872 | tf_op jit(solution)/shard_map/ppermute | solution.py:64
  175.5 15.4 %collective-permute-start.17 = (bf16[512,512]{0,1:T(8,128)(2,1)S(1)}, bf16[512,512]{0,1:T(8,128)(2,1)S(1)}, u32[]{:S(2)}, u32[]{:S(2)}) collective-permute-start(bf16[512,512]{0,1:T(8,128)(2,1)S(1)} %pad_maximum_fusion.19), channel_id=1, source_target_pairs={{0,1},{1,0},{2,3},{3,2},{4,5},{5,4},{6,7},{7,6},{8,9},{9,8},{10,11... | collective-permute-start | bytes 1572872 | tf_op jit(solution)/shard_map/ppermute | solution.py:64
  182.3 11.9 %collective-permute-start.22 = (bf16[256,1024]{0,1:T(8,128)(2,1)S(1)}, bf16[256,1024]{0,1:T(8,128)(2,1)S(1)}, u32[]{:S(2)}, u32[]{:S(2)}) collective-permute-start(bf16[256,1024]{0,1:T(8,128)(2,1)S(1)} %constant_dynamic-slice_fusion.13), channel_id=1, source_target_pairs={{0,1},{1,0},{2,3},{3,2},{4,5},{5,4},{6,7},{7,6},{8,9},{9,8},{10,11... | collective-permute-start | bytes 1572872 | tf_op jit(solution)/shard_map/ppermute | solution.py:64
  184.2 46.7 %collective-permute-start.72 = (bf16[4,128,1024]{2,1,0:T(8,128)(2,1)}, bf16[4,128,1024]{2,1,0:T(8,128)(2,1)}, u32[]{:S(2)}, u32[]{:S(2)}) collective-permute-start(bf16[4,128,1024]{2,1,0:T(8,128)(2,1)} %dynamic-slice_bitcast_fusion), channel_id=1, source_target_pairs={{0,4},{4,0},{8,12},{12,8},{16,20},{20,16},{24,28},{28,24},{1,5},{5... | collective-permute-start | bytes 3145736 | tf_op jit(solution)/shard_map/ppermute | solution.py:64
  190.9 44.3 %collective-permute-start.66 = (bf16[4,128,1024]{2,1,0:T(8,128)(2,1)}, bf16[4,128,1024]{2,1,0:T(8,128)(2,1)}, u32[]{:S(2)}, u32[]{:S(2)}) collective-permute-start(bf16[4,128,1024]{2,1,0:T(8,128)(2,1)} %dynamic-slice_bitcast_fusion.2), channel_id=1, source_target_pairs={{0,4},{4,0},{8,12},{12,8},{16,20},{20,16},{24,28},{28,24},{1,5},{5... | collective-permute-start | bytes 3145736 | tf_op jit(solution)/shard_map/ppermute | solution.py:64
  191.6 63.4 %collective-permute-start.69 = (bf16[4,128,1024]{2,1,0:T(8,128)(2,1)}, bf16[4,128,1024]{2,1,0:T(8,128)(2,1)}, u32[]{:S(2)}, u32[]{:S(2)}) collective-permute-start(bf16[4,128,1024]{2,1,0:T(8,128)(2,1)} %dynamic-slice_bitcast_fusion.1), channel_id=1, source_target_pairs={{0,4},{4,0},{8,12},{12,8},{16,20},{20,16},{24,28},{28,24},{1,5},{5... | collective-permute-start | bytes 3145736 | tf_op jit(solution)/shard_map/ppermute | solution.py:64
  194.2 14.1 %collective-permute-start.7 = (bf16[512,256]{0,1:T(8,128)(2,1)S(1)}, bf16[512,256]{0,1:T(8,128)(2,1)S(1)}, u32[]{:S(2)}, u32[]{:S(2)}) collective-permute-start(bf16[512,256]{0,1:T(8,128)(2,1)S(1)} %dynamic-slice_convert_fusion.13), channel_id=1, source_target_pairs={{0,2},{1,3},{2,0},{3,1},{4,6},{5,7},{6,4},{7,5},{8,10},{9,11},{10,... | collective-permute-start | bytes 786440 | tf_op jit(solution)/shard_map/ppermute | solution.py:64
  202.7 17.0 %collective-permute-start.26 = (bf16[256,1024]{0,1:T(8,128)(2,1)S(1)}, bf16[256,1024]{0,1:T(8,128)(2,1)}, u32[]{:S(2)}, u32[]{:S(2)}) collective-permute-start(bf16[256,1024]{0,1:T(8,128)(2,1)S(1)} %add_convert_fusion.7), channel_id=1, source_target_pairs={{0,2},{1,3},{2,0},{3,1},{4,6},{5,7},{6,4},{7,5},{8,10},{9,11},{10,... | collective-permute-start | bytes 1572872 | tf_op jit(solution)/shard_map/ppermute | solution.py:64
  208.3 21.2 %collective-permute-start.23 = (bf16[256,1024]{0,1:T(8,128)(2,1)}, bf16[256,1024]{0,1:T(8,128)(2,1)}, u32[]{:S(2)}, u32[]{:S(2)}) collective-permute-start(bf16[256,1024]{0,1:T(8,128)(2,1)} %add_convert_fusion.9), channel_id=1, source_target_pairs={{0,2},{1,3},{2,0},{3,1},{4,6},{5,7},{6,4},{7,5},{8,10},{9,11},{10,... | collective-permute-start | bytes 1572872 | tf_op jit(solution)/shard_map/ppermute | solution.py:64
  220.8 39.7 %collective-permute-start.27 = (bf16[256,1024]{0,1:T(8,128)(2,1)S(1)}, bf16[256,1024]{0,1:T(8,128)(2,1)S(1)}, u32[]{:S(2)}, u32[]{:S(2)}) collective-permute-start(bf16[256,1024]{0,1:T(8,128)(2,1)S(1)} %add_convert_fusion.6), channel_id=1, source_target_pairs={{0,1},{1,0},{2,3},{3,2},{4,5},{5,4},{6,7},{7,6},{8,9},{9,8},{10,11... | collective-permute-start | bytes 1572872 | tf_op jit(solution)/shard_map/ppermute | solution.py:64
  230.8 29.8 %collective-permute-start.24 = (bf16[256,1024]{0,1:T(8,128)(2,1)S(1)}, bf16[256,1024]{0,1:T(8,128)(2,1)S(1)}, u32[]{:S(2)}, u32[]{:S(2)}) collective-permute-start(bf16[256,1024]{0,1:T(8,128)(2,1)S(1)} %add_convert_fusion.8), channel_id=1, source_target_pairs={{0,1},{1,0},{2,3},{3,2},{4,5},{5,4},{6,7},{7,6},{8,9},{9,8},{10,11... | collective-permute-start | bytes 1572872 | tf_op jit(solution)/shard_map/ppermute | solution.py:64
  233.7 153.3 %collective-permute-start.73 = (bf16[2,128,1024]{2,1,0:T(8,128)(2,1)}, bf16[2,128,1024]{2,1,0:T(8,128)(2,1)}, u32[]{:S(2)}, u32[]{:S(2)}) collective-permute-start(bf16[2,128,1024]{2,1,0:T(8,128)(2,1)} %fusion.134), channel_id=1, source_target_pairs={{0,8},{4,12},{8,0},{12,4},{16,24},{20,28},{24,16},{28,20},{1,9},{5... | collective-permute-start | bytes 1572872 | tf_op jit(solution)/shard_map/ppermute | solution.py:64
  237.9 151.0 %collective-permute-start.67 = (bf16[2,128,1024]{2,1,0:T(8,128)(2,1)}, bf16[2,128,1024]{2,1,0:T(8,128)(2,1)}, u32[]{:S(2)}, u32[]{:S(2)}) collective-permute-start(bf16[2,128,1024]{2,1,0:T(8,128)(2,1)} %fusion.133), channel_id=1, source_target_pairs={{0,8},{4,12},{8,0},{12,4},{16,24},{20,28},{24,16},{28,20},{1,9},{5... | collective-permute-start | bytes 1572872 | tf_op jit(solution)/shard_map/ppermute | solution.py:64
  259.0 133.9 %collective-permute-start.70 = (bf16[2,128,1024]{2,1,0:T(8,128)(2,1)}, bf16[2,128,1024]{2,1,0:T(8,128)(2,1)}, u32[]{:S(2)}, u32[]{:S(2)}) collective-permute-start(bf16[2,128,1024]{2,1,0:T(8,128)(2,1)} %fusion.135), channel_id=1, source_target_pairs={{0,8},{4,12},{8,0},{12,4},{16,24},{20,28},{24,16},{28,20},{1,9},{5... | collective-permute-start | bytes 1572872 | tf_op jit(solution)/shard_map/ppermute | solution.py:64
  338.0 56.8 %collective-permute-start.57 = (bf16[4,128,256]{2,1,0:T(8,128)(2,1)}, bf16[4,128,256]{2,1,0:T(8,128)(2,1)}, u32[]{:S(2)}, u32[]{:S(2)}) collective-permute-start(bf16[4,128,256]{2,1,0:T(8,128)(2,1)} %dynamic-slice_bitcast_fusion.12), channel_id=1, source_target_pairs={{0,4},{4,0},{8,12},{12,8},{16,20},{20,16},{24,28},{28,24},{1,5},{5... | collective-permute-start | bytes 786440 | tf_op jit(solution)/shard_map/ppermute | solution.py:64
  350.0 88.1 %collective-permute-start.31 = (bf16[1024,512]{0,1:T(8,128)(2,1)}, bf16[1024,512]{0,1:T(8,128)(2,1)}, u32[]{:S(2)}, u32[]{:S(2)}) collective-permute-start(bf16[1024,512]{0,1:T(8,128)(2,1)} %pad_maximum_fusion.12), channel_id=1, source_target_pairs={{0,1},{1,0},{2,3},{3,2},{4,5},{5,4},{6,7},{7,6},{8,9},{9,8},{10,11... | collective-permute-start | bytes 3145736 | tf_op jit(solution)/shard_map/ppermute | solution.py:64
  387.0 35.5 %collective-permute-start.28 = (bf16[256,1024]{0,1:T(8,128)(2,1)}, bf16[256,1024]{0,1:T(8,128)(2,1)S(1)}, u32[]{:S(2)}, u32[]{:S(2)}) collective-permute-start(bf16[256,1024]{0,1:T(8,128)(2,1)} %constant_dynamic-slice_fusion.11), channel_id=1, source_target_pairs={{0,1},{1,0},{2,3},{3,2},{4,5},{5,4},{6,7},{7,6},{8,9},{9,8},{10,11... | collective-permute-start | bytes 1572872 | tf_op jit(solution)/shard_map/ppermute | solution.py:64
  388.9 27.0 %collective-permute-start.74 = (bf16[1,128,1024]{2,1,0:T(8,128)(2,1)S(1)}, bf16[1,128,1024]{2,1,0:T(8,128)(2,1)S(1)}, u32[]{:S(2)}, u32[]{:S(2)}) collective-permute-start(bf16[1,128,1024]{2,1,0:T(8,128)(2,1)S(1)} %dynamic-slice_convert_fusion.6), channel_id=1, source_target_pairs={{0,16},{4,20},{8,24},{12,28},{16,0},{20,4},{24,8},{28,12},{1,17},{... | collective-permute-start | bytes 786440 | tf_op jit(solution)/shard_map/ppermute | solution.py:64
  392.9 28.7 %collective-permute-start.68 = (bf16[1,128,1024]{2,1,0:T(8,128)(2,1)S(1)}, bf16[1,128,1024]{2,1,0:T(8,128)(2,1)S(1)}, u32[]{:S(2)}, u32[]{:S(2)}) collective-permute-start(bf16[1,128,1024]{2,1,0:T(8,128)(2,1)S(1)} %dynamic-slice_convert_fusion.8), channel_id=1, source_target_pairs={{0,16},{4,20},{8,24},{12,28},{16,0},{20,4},{24,8},{28,12},{1,17},{... | collective-permute-start | bytes 786440 | tf_op jit(solution)/shard_map/ppermute | solution.py:64
  394.7 31.6 %collective-permute-start.71 = (bf16[1,128,1024]{2,1,0:T(8,128)(2,1)S(1)}, bf16[1,128,1024]{2,1,0:T(8,128)(2,1)S(1)}, u32[]{:S(2)}, u32[]{:S(2)}) collective-permute-start(bf16[1,128,1024]{2,1,0:T(8,128)(2,1)S(1)} %dynamic-slice_convert_fusion.7), channel_id=1, source_target_pairs={{0,16},{4,20},{8,24},{12,28},{16,0},{20,4},{24,8},{28,12},{1,17},{... | collective-permute-start | bytes 786440 | tf_op jit(solution)/shard_map/ppermute | solution.py:64
  415.9 14.5 %collective-permute-start.58 = (bf16[2,128,256]{2,1,0:T(8,128)(2,1)S(1)}, bf16[2,128,256]{2,1,0:T(8,128)(2,1)S(1)}, u32[]{:S(2)}, u32[]{:S(2)}) collective-permute-start(bf16[2,128,256]{2,1,0:T(8,128)(2,1)S(1)} %fusion.147), channel_id=1, source_target_pairs={{0,8},{4,12},{8,0},{12,4},{16,24},{20,28},{24,16},{28,20},{1,9},{5... | collective-permute-start | bytes 393224 | tf_op jit(solution)/shard_map/ppermute | solution.py:64
  423.4 12.5 %collective-permute-start.29 = (bf16[256,1024]{0,1:T(8,128)(2,1)}, bf16[256,1024]{0,1:T(8,128)(2,1)}, u32[]{:S(2)}, u32[]{:S(2)}) collective-permute-start(bf16[256,1024]{0,1:T(8,128)(2,1)} %add_convert_fusion.5), channel_id=1, source_target_pairs={{0,2},{1,3},{2,0},{3,1},{4,6},{5,7},{6,4},{7,5},{8,10},{9,11},{10,... | collective-permute-start | bytes 1572872 | tf_op jit(solution)/shard_map/ppermute | solution.py:64
  442.2 51.6 %collective-permute-start.32 = (bf16[1024,256]{0,1:T(8,128)(2,1)}, bf16[1024,256]{0,1:T(8,128)(2,1)}, u32[]{:S(2)}, u32[]{:S(2)}) collective-permute-start(bf16[1024,256]{0,1:T(8,128)(2,1)} %dynamic-slice_convert_fusion.5), channel_id=1, source_target_pairs={{0,2},{1,3},{2,0},{3,1},{4,6},{5,7},{6,4},{7,5},{8,10},{9,11},{10,... | collective-permute-start | bytes 1572872 | tf_op jit(solution)/shard_map/ppermute | solution.py:64
  465.1 30.4 %collective-permute-start.33 = (bf16[512,512]{0,1:T(8,128)(2,1)}, bf16[512,512]{0,1:T(8,128)(2,1)}, u32[]{:S(2)}, u32[]{:S(2)}) collective-permute-start(bf16[512,512]{0,1:T(8,128)(2,1)} %pad_maximum_fusion.21), channel_id=1, source_target_pairs={{0,1},{1,0},{2,3},{3,2},{4,5},{5,4},{6,7},{7,6},{8,9},{9,8},{10,11... | collective-permute-start | bytes 1572872 | tf_op jit(solution)/shard_map/ppermute | solution.py:64
  473.8 93.8 %collective-permute-start.63 = (bf16[4,128,1024]{2,1,0:T(8,128)(2,1)}, bf16[4,128,1024]{2,1,0:T(8,128)(2,1)}, u32[]{:S(2)}, u32[]{:S(2)}) collective-permute-start(bf16[4,128,1024]{2,1,0:T(8,128)(2,1)} %dynamic-slice_bitcast_fusion.3), channel_id=1, source_target_pairs={{0,4},{4,0},{8,12},{12,8},{16,20},{20,16},{24,28},{28,24},{1,5},{5... | collective-permute-start | bytes 3145736 | tf_op jit(solution)/shard_map/ppermute | solution.py:64
  492.4 73.3 %collective-permute-start.60 = (bf16[4,128,1024]{2,1,0:T(8,128)(2,1)}, bf16[4,128,1024]{2,1,0:T(8,128)(2,1)}, u32[]{:S(2)}, u32[]{:S(2)}) collective-permute-start(bf16[4,128,1024]{2,1,0:T(8,128)(2,1)} %bitcast.564), channel_id=1, source_target_pairs={{0,4},{4,0},{8,12},{12,8},{16,20},{20,16},{24,28},{28,24},{1,5},{5... | collective-permute-start | bytes 3145736 | tf_op jit(solution)/shard_map/ppermute | solution.py:64
  549.6 21.3 %collective-permute-start.48 = (bf16[4,128,256]{2,1,0:T(8,128)(2,1)}, bf16[4,128,256]{2,1,0:T(8,128)(2,1)}, u32[]{:S(2)}, u32[]{:S(2)}) collective-permute-start(bf16[4,128,256]{2,1,0:T(8,128)(2,1)} %dynamic-slice_bitcast_fusion.13), channel_id=1, source_target_pairs={{0,4},{4,0},{8,12},{12,8},{16,20},{20,16},{24,28},{28,24},{1,5},{5... | collective-permute-start | bytes 786440 | tf_op jit(solution)/shard_map/ppermute | solution.py:64
  550.3 22.6 %collective-permute-start.42 = (bf16[4,128,256]{2,1,0:T(8,128)(2,1)}, bf16[4,128,256]{2,1,0:T(8,128)(2,1)}, u32[]{:S(2)}, u32[]{:S(2)}) collective-permute-start(bf16[4,128,256]{2,1,0:T(8,128)(2,1)} %dynamic-slice_bitcast_fusion.15), channel_id=1, source_target_pairs={{0,4},{4,0},{8,12},{12,8},{16,20},{20,16},{24,28},{28,24},{1,5},{5... | collective-permute-start | bytes 786440 | tf_op jit(solution)/shard_map/ppermute | solution.py:64
  551.8 13.3 %collective-permute-start.39 = (f32[20,1024]{1,0:T(8,128)S(1)}, f32[20,1024]{1,0:T(8,128)S(1)}, u32[]{:S(2)}, u32[]{:S(2)}) collective-permute-start(f32[20,1024]{1,0:T(8,128)S(1)} %add.764), channel_id=1, source_target_pairs={{0,4},{4,0},{8,12},{12,8},{16,20},{20,16},{24,28},{28,24},{1,5},{5... | collective-permute-start | bytes 245768 | tf_op jit(solution)/shard_map/ppermute | solution.py:64
  565.7 58.8 %collective-permute-start.35 = (bf16[1024,512]{0,1:T(8,128)(2,1)}, bf16[1024,512]{0,1:T(8,128)(2,1)S(1)}, u32[]{:S(2)}, u32[]{:S(2)}) collective-permute-start(bf16[1024,512]{0,1:T(8,128)(2,1)} %pad_maximum_fusion.13), channel_id=1, source_target_pairs={{0,1},{1,0},{2,3},{3,2},{4,5},{5,4},{6,7},{7,6},{8,9},{9,8},{10,11... | collective-permute-start | bytes 3145736 | tf_op jit(solution)/shard_map/ppermute | solution.py:64
  571.0 48.8 %collective-permute-start.64 = (bf16[2,128,1024]{2,1,0:T(8,128)(2,1)S(1)}, bf16[2,128,1024]{2,1,0:T(8,128)(2,1)S(1)}, u32[]{:S(2)}, u32[]{:S(2)}) collective-permute-start(bf16[2,128,1024]{2,1,0:T(8,128)(2,1)S(1)} %fusion.132), channel_id=1, source_target_pairs={{0,8},{4,12},{8,0},{12,4},{16,24},{20,28},{24,16},{28,20},{1,9},{5... | collective-permute-start | bytes 1572872 | tf_op jit(solution)/shard_map/ppermute | solution.py:64
  572.9 50.6 %collective-permute-start.61 = (bf16[2,128,1024]{2,1,0:T(8,128)(2,1)S(1)}, bf16[2,128,1024]{2,1,0:T(8,128)(2,1)S(1)}, u32[]{:S(2)}, u32[]{:S(2)}) collective-permute-start(bf16[2,128,1024]{2,1,0:T(8,128)(2,1)S(1)} %fusion.131), channel_id=1, source_target_pairs={{0,8},{4,12},{8,0},{12,4},{16,24},{20,28},{24,16},{28,20},{1,9},{5... | collective-permute-start | bytes 1572872 | tf_op jit(solution)/shard_map/ppermute | solution.py:64
  575.2 24.7 %collective-permute-start.49 = (bf16[2,128,256]{2,1,0:T(8,128)(2,1)S(1)}, bf16[2,128,256]{2,1,0:T(8,128)(2,1)S(1)}, u32[]{:S(2)}, u32[]{:S(2)}) collective-permute-start(bf16[2,128,256]{2,1,0:T(8,128)(2,1)S(1)} %fusion.149), channel_id=1, source_target_pairs={{0,8},{4,12},{8,0},{12,4},{16,24},{20,28},{24,16},{28,20},{1,9},{5... | collective-permute-start | bytes 393224 | tf_op jit(solution)/shard_map/ppermute | solution.py:64
  576.2 26.5 %collective-permute-start.43 = (bf16[2,128,256]{2,1,0:T(8,128)(2,1)S(1)}, bf16[2,128,256]{2,1,0:T(8,128)(2,1)S(1)}, u32[]{:S(2)}, u32[]{:S(2)}) collective-permute-start(bf16[2,128,256]{2,1,0:T(8,128)(2,1)S(1)} %fusion.146), channel_id=1, source_target_pairs={{0,8},{4,12},{8,0},{12,4},{16,24},{20,28},{24,16},{28,20},{1,9},{5... | collective-permute-start | bytes 393224 | tf_op jit(solution)/shard_map/ppermute | solution.py:64
  620.0 18.3 %collective-permute-start.65 = (bf16[1,128,1024]{2,1,0:T(8,128)(2,1)S(1)}, bf16[1,128,1024]{2,1,0:T(8,128)(2,1)S(1)}, u32[]{:S(2)}, u32[]{:S(2)}) collective-permute-start(bf16[1,128,1024]{2,1,0:T(8,128)(2,1)S(1)} %dynamic-slice_convert_fusion.9), channel_id=1, source_target_pairs={{0,16},{4,20},{8,24},{12,28},{16,0},{20,4},{24,8},{28,12},{1,17},{... | collective-permute-start | bytes 786440 | tf_op jit(solution)/shard_map/ppermute | solution.py:64
  624.4 19.2 %collective-permute-start.62 = (bf16[1,128,1024]{2,1,0:T(8,128)(2,1)}, bf16[1,128,1024]{2,1,0:T(8,128)(2,1)S(1)}, u32[]{:S(2)}, u32[]{:S(2)}) collective-permute-start(bf16[1,128,1024]{2,1,0:T(8,128)(2,1)} %dynamic-slice_convert_fusion.10), channel_id=1, source_target_pairs={{0,16},{4,20},{8,24},{12,28},{16,0},{20,4},{24,8},{28,12},{1,17},{... | collective-permute-start | bytes 786440 | tf_op jit(solution)/shard_map/ppermute | solution.py:64
  625.9 18.6 %collective-permute-start.36 = (bf16[1024,256]{0,1:T(8,128)(2,1)}, bf16[1024,256]{0,1:T(8,128)(2,1)}, u32[]{:S(2)}, u32[]{:S(2)}) collective-permute-start(bf16[1024,256]{0,1:T(8,128)(2,1)} %dynamic-slice_convert_fusion.4), channel_id=1, source_target_pairs={{0,2},{1,3},{2,0},{3,1},{4,6},{5,7},{6,4},{7,5},{8,10},{9,11},{10,... | collective-permute-start | bytes 1572872 | tf_op jit(solution)/shard_map/ppermute | solution.py:64
  (216 other events, 1581.1 us)
